TPU v7x, 32 devices: a whole 2x2x4 slice. The times are simulated.
32 devices in a mesh: wide: 8 (over y, x, core), narrow: 4 (over z).
Axes of the slice: x: 2, y: 2, z: 4, core: 2. Of those that a mesh axis runs over, the one named last changes fastest.
Arguments:
- amplitudes: bfloat16 [256, 4, 4096], P('wide', None, 'narrow'), may hold values from -6 to 6
- amp_tiles: int32 [8, 4], replicated, may hold values from 0 to 7, all different within a row
- integrals: bfloat16 [8, 2, 4096, 4096], P('wide', None, None, 'narrow'), may hold values from -0.09375 to 0.09375
- cd_tiles: int32 [8, 2], replicated, may hold values from 0 to 7, all different within a row
- q_owner: int32 [8], replicated, may hold values from 0 to 7, each once
Outputs:
- residual: bfloat16 [256, 8, 4096], P('wide', None, 'narrow')
Inputs may be any that keep to these rules, and one draw needn't show every extreme that they name: `amp_tiles`: within a row, the 4 tiles are different. `cd_tiles`: within a row, the 2 tiles are different; every tile is named by some row. `q_owner`: each owner index appears once.
All inputs are finite; a program needn't handle non-finite values.
Results may differ from a plain program's by a relative error of at most 0.017.
Values may be sent and summed in bfloat16 or wider, within the bound.
No kernel may reach another device: no remote copies, remote signals or barrier semaphores. Data moves between devices by JAX's collectives and lax.ppermute only.
A program may use at most 64 MiB of HBM per device.

v0:
```python
import functools

import jax
import jax.numpy as jnp
from jax import lax
from jax.experimental import pallas as pl
from jax.experimental.pallas import tpu as pltpu
from jax.sharding import PartitionSpec as P

PART = 512
PIECE = 256
LIMIT = 48 << 20


def pick_kernel(peers, amp_tiles, cd_tiles, q_owner, amps, *rest):
    own, mate, *outs = rest[: peers // 2 + 1]
    held, slots = rest[peers // 2 + 1 :]
    width = amps.shape[1]
    wants = cd_tiles.shape[0]
    me = lax.axis_index("wide")

    def look(q, carry):
        peer = q_owner[q] ^ me
        for k in range(wants):
            slot = jnp.int32(width)
            for t in range(width):
                slot = jnp.where(amp_tiles[t, me] == cd_tiles[k, q], t, slot)
            slots[peer, k] = slot
        return carry

    lax.fori_loop(0, peers, look, 0)
    for t in range(width):
        held[t] = amps[:, t, :]
    held[width] = jnp.zeros_like(held[width])
    for j in range(peers):
        for k in range(wants):
            into = (own, mate)[j].at[k] if j < 2 else outs[j // 2 - 1].at[j % 2, k]
            into[...] = held[slots[j, k]]


def pick(amplitudes, amp_tiles, cd_tiles, q_owner):
    rows, width, depth = amplitudes.shape
    peers, wants = cd_tiles.shape
    smem = pl.BlockSpec(memory_space=pltpu.SMEM)
    vmem = pl.BlockSpec(memory_space=pltpu.VMEM)
    return pl.pallas_call(
        functools.partial(pick_kernel, peers),
        out_shape=[jax.ShapeDtypeStruct((wants, rows, depth), jnp.bfloat16)] * 2
        + [jax.ShapeDtypeStruct((2, wants, rows, depth), jnp.bfloat16)] * (peers // 2 - 1),
        in_specs=[smem, smem, smem, vmem],
        out_specs=[vmem] * (peers // 2 + 1),
        scratch_shapes=[
            pltpu.VMEM((width + 1, rows, depth), jnp.bfloat16),
            pltpu.SMEM((peers, wants), jnp.int32),
        ],
        compiler_params=pltpu.CompilerParams(vmem_limit_bytes=LIMIT),
        name="pick",
    )(amp_tiles.T, cd_tiles.T, q_owner, amplitudes)


def product_kernel(halves, chunks, rows, order, shard, *refs):
    refs = list(refs)
    picked = [refs.pop(0) for _ in range(len(halves))]
    ints = refs.pop(0)
    outs = [refs.pop(0) for _ in range(chunks)]
    buffer, turned, padded, sems = refs
    shares, wants, share, depth = buffer.shape
    pieces = sems.shape[2]
    piece = share // pieces

    def copy(s, k, p):
        start = pl.multiple_of(shard[order[s]] * share, share) + p * piece
        return pltpu.make_async_copy(
            ints.at[0, k, pl.ds(start, piece), :], buffer.at[s, k, pl.ds(p * piece, piece), :], sems.at[s, k, p]
        )

    for s in range(shares):
        for p in range(pieces):
            for k in range(wants):
                copy(s, k, p).start()

    padded[...] = jnp.zeros_like(padded)
    for k in range(wants):
        for i, (ref, half) in enumerate(zip(picked, halves)):
            padded[i * rows : (i + 1) * rows, :] = ref[k] if half is None else ref[half, k]
        turned[k] = padded[...].T

    each = len(halves) * rows // chunks
    part = min(PART, share)
    for s in range(shares):
        for i in range(share // part):
            at = slice(i * part, (i + 1) * part)
            for p in range(i * part // piece, (i + 1) * part // piece):
                for k in range(wants):
                    copy(s, k, p).wait()
            total = None
            for k in range(wants):
                term = jnp.dot(buffer[s, k, at, :], turned[k], preferred_element_type=jnp.float32)
                total = term if total is None else total + term
            total = total.T.astype(jnp.bfloat16)
            for c in range(chunks):
                outs[c][s, :, at] = total[c * each : (c + 1) * each]


def product(shard, order, picked, ints, rows, chunks):
    arrays, halves = [p for p, _ in picked], [h for _, h in picked]
    _, wants, pairs, depth = ints.shape
    share = pairs // shard.shape[0]
    count = len(picked)
    lanes = -(-count * rows // 128) * 128
    each = count * rows // chunks
    shares = len(order)
    pieces = max(1, share // PIECE)
    vmem = pl.BlockSpec(memory_space=pltpu.VMEM)
    return pl.pallas_call(
        functools.partial(product_kernel, halves, chunks, rows, order),
        out_shape=[jax.ShapeDtypeStruct((shares, each, share), jnp.bfloat16)] * chunks,
        in_specs=[pl.BlockSpec(memory_space=pltpu.SMEM)] + [vmem] * count + [pl.BlockSpec(memory_space=pl.ANY)],
        out_specs=[vmem] * chunks,
        scratch_shapes=[
            pltpu.VMEM((shares, wants, share, depth), jnp.bfloat16),
            pltpu.VMEM((wants, depth, lanes), jnp.bfloat16),
            pltpu.VMEM((lanes, depth), jnp.bfloat16),
            pltpu.SemaphoreType.DMA((shares, wants, pieces)),
        ],
        compiler_params=pltpu.CompilerParams(vmem_limit_bytes=LIMIT),
        cost_estimate=pl.CostEstimate(
            flops=2 * 256 * wants * depth * share * shares,
            bytes_accessed=2 * wants * depth * share * shares,
            transcendentals=0,
        ),
        name="product",
    )(shard, *arrays, ints)


def add(*terms):
    return sum(t.astype(jnp.float32) for t in terms).astype(jnp.bfloat16)


def order_kernel(peers, halves, q_owner, *refs):
    shares, out, held = refs[:peers], refs[peers], refs[peers + 1]
    me = lax.axis_index("wide")

    def tile_of(j):
        def look(q, found):
            return jnp.where(q_owner[q] == me ^ j, q, found)

        return lax.fori_loop(0, peers, look, jnp.int32(0))

    for j in range(peers):
        held[tile_of(j)] = shares[j][...] if halves[j] is None else shares[j][halves[j]]
    for q in range(peers):
        out[:, q, :] = held[q]


def order(q_owner, shares, rows):
    peers = len(shares)
    share = shares[0][0].shape[-1]
    vmem = pl.BlockSpec(memory_space=pltpu.VMEM)
    return pl.pallas_call(
        functools.partial(order_kernel, peers, [h for _, h in shares]),
        out_shape=jax.ShapeDtypeStruct((rows, peers, share), jnp.bfloat16),
        in_specs=[pl.BlockSpec(memory_space=pltpu.SMEM)] + [vmem] * peers,
        out_specs=vmem,
        scratch_shapes=[pltpu.VMEM((peers, rows, share), jnp.bfloat16)],
        compiler_params=pltpu.CompilerParams(vmem_limit_bytes=LIMIT),
        name="order",
    )(q_owner, *[s for s, _ in shares])


def on_device(amplitudes, amp_tiles, integrals, cd_tiles, q_owner):
    peers = lax.axis_size("wide")
    devices = lax.axis_size("narrow")
    rows = amplitudes.shape[0]
    at = lax.axis_index("narrow")

    gray = at ^ (at >> 1)
    code = jnp.arange(devices, dtype=jnp.int32) ^ gray
    shard, shift = code, code >> 1
    for _ in range(devices.bit_length() - 2):
        shard, shift = shard ^ shift, shift >> 1
    odd, even = tuple(range(1, devices, 2)), tuple(range(0, devices, 2))

    def swap(value, j):
        return lax.ppermute(value, "wide", [(w, w ^ j) for w in range(peers)])

    def swap_line(value, mask):
        return lax.ppermute(value, "narrow", [(n, n ^ mask) for n in range(devices)])

    mine, mate, *picked = pick(amplitudes, amp_tiles, cd_tiles, q_owner)
    mate = swap(mate, 1)
    arrived = [None] + [swap(picked[g - 1], 2 * g) for g in range(1, peers // 2)]
    handed = [None] + [swap(arrived[g][1], 1) for g in range(1, peers // 2)]
    first = [(mine, None), (mate, None)]
    rest = [pair for g in range(1, peers // 2) for pair in ((arrived[g], 0), (handed[g], None))]

    def totals(group, chunks):
        away = product(shard, odd, group, integrals, rows, chunks)
        keep = product(shard, even, group, integrals, rows, chunks)
        results = []
        for c in range(chunks):
            terms = {2 * i: [keep[c][i]] for i in range(devices // 2)}
            message, names = away[c], list(range(1, devices, 2))
            step = 0
            while True:
                got = swap_line(message, (2 << step) - 1)
                for i, r in enumerate(names):
                    terms[r ^ (1 << step)].append(got[i])
                step += 1
                if 1 << step == devices:
                    break
                names = [r for r in sorted(terms) if r >> step & 1]
                message = jnp.stack([add(*terms.pop(r)) for r in names])
            results.append(add(*terms[0]).reshape(2, rows, -1))
        return results

    own, = totals(first, 1)
    shares = [(own, 0), (swap(own[1], 1), None)]
    for g, total in enumerate(totals(rest, peers // 2 - 1), 1):
        got = swap(total, 2 * g)
        shares += [(got, 0), (swap(got[1], 1), None)]
    return order(q_owner, shares, rows)


def solution(mesh):
    placed = (P("wide", None, "narrow"), P(), P("wide", None, None, "narrow"), P(), P())
    return jax.shard_map(
        on_device, mesh=mesh, in_specs=placed, out_specs=P("wide", None, "narrow"), check_vma=False
    )
```

profile of v0, /device:TPU:0, one launch (start us, length us, event | category | flops | bytes accessed | tf_op | source)
XLA Modules:
  0.0 75.3 jit_solution(17505957170570634995)
XLA Ops:
  0.0 0.9 %copy-done = bf16[32,4,1024]{2,1,0:T(4,128)(2,1)S(1)} copy-done((bf16[32,4,1024]{2,1,0:T(4,128)(2,1)S(1)}, bf16[32,4,1024]{2,1,0:T(4,128)(2,1)}, u32[]{:S(2)}) %copy-start) | copy-done | bytes 262168
  1.0 0.7 copy-done.1
  1.6 0.7 copy-done.2
  2.3 0.7 copy-done.4
  3.0 1.4 %pick.1 = (bf16[2,32,1024]{2,1,0:T(8,128)(2,1)S(1)}, bf16[2,32,1024]{2,1,0:T(8,128)(2,1)S(1)}, bf16[2,2,32,1024]{3,2,1,0:T(8,128)(2,1)S(1)}, bf16[2,2,32,1024]{3...) custom-call(s32[4,8]{1,0:T(4,128)S(1)} %bitcast.21, s32[2,8]{1,0:T(2,128)S(1)} %bitcast.22, s32[8]{0:T(128)S(1)} %copy-done.2, ...), custom_call_target="tpu_custom_call" | custom-call | tf_op jit(solution)/shard_map/pick/pallas_call | solution.py:46
  4.3 0.5 collective-permute-start
  4.8 2.6 %collective-permute-start.4 = (bf16[2,2,32,1024]{3,2,1,0:T(8,128)(2,1)S(1)}, bf16[2,2,32,1024]{3,2,1,0:T(8,128)(2,1)S(1)}, u32[]{:S(2)}, u32[]{:S(2)}) collective-permute-start(bf16[2,2,32,1024]{3,2,1,0:T(8,128)(2,1)S(1)} %get-tuple-element.18), channel_id=1, source_target_pairs={{0,8},{4,12},{8,0},{12,4},{16,24},{20,28},{24,16},{28,20},{1,9},{5... | collective-permute-start | bytes 786440 | tf_op jit(solution)/shard_map/ppermute | solution.py:185
  7.4 1.5 %collective-permute-start.6 = (bf16[2,2,32,1024]{3,2,1,0:T(8,128)(2,1)S(1)}, bf16[2,2,32,1024]{3,2,1,0:T(8,128)(2,1)S(1)}, u32[]{:S(2)}, u32[]{:S(2)}) collective-permute-start(bf16[2,2,32,1024]{3,2,1,0:T(8,128)(2,1)S(1)} %get-tuple-element.19), channel_id=1, source_target_pairs={{0,16},{4,20},{8,24},{12,28},{16,0},{20,4},{24,8},{28,12},{1,17},{... | collective-permute-start | bytes 786440 | tf_op jit(solution)/shard_map/ppermute | solution.py:185
  8.9 0.0 collective-permute-start.8
  9.0 7.3 %product.5 = bf16[2,64,1024]{2,1,0:T(8,128)(2,1)S(1)} custom-call(s32[4]{0:T(128)S(1)} %shift-right-arithmetic_xor_fusion.shard, bf16[2,32,1024]{2,1,0:T(8,128)(2,1)S(1)} %get-tuple-element.16.refs_0_, bf16[2,32,1024]{2,1,0:T(8,128)(2,1)S(1)} %collective-permute-done.refs_1_, bf16[1,2,4096,1024]{3,2,1,0:T(8,128)(2,1)} %refs_6_.3), custom_call_target="tpu_custom_call" | custom-call | flops 2147483648 | bytes 8388608 | tf_op jit(solution)/shard_map/product/pallas_call | solution.py:115
  16.3 2.1 %collective-permute-start.1 = (bf16[2,64,1024]{2,1,0:T(8,128)(2,1)S(1)}, bf16[2,64,1024]{2,1,0:T(8,128)(2,1)S(1)}, u32[]{:S(2)}, u32[]{:S(2)}) collective-permute-start(bf16[2,64,1024]{2,1,0:T(8,128)(2,1)S(1)} %product.5), channel_id=1, source_target_pairs={{0,1},{1,0},{2,3},{3,2},{4,5},{5,4},{6,7},{7,6},{8,9},{9,8},{10,11... | collective-permute-start | bytes 786440 | tf_op jit(solution)/shard_map/ppermute | solution.py:188
  18.4 7.3 %product.4 = bf16[2,64,1024]{2,1,0:T(8,128)(2,1)S(1)} custom-call(s32[4]{0:T(128)S(1)} %shift-right-arithmetic_xor_fusion.shard, bf16[2,32,1024]{2,1,0:T(8,128)(2,1)S(1)} %get-tuple-element.16.refs_0_, bf16[2,32,1024]{2,1,0:T(8,128)(2,1)S(1)} %collective-permute-done.refs_1_, bf16[1,2,4096,1024]{3,2,1,0:T(8,128)(2,1)} %refs_6_.3), custom_call_target="tpu_custom_call" | custom-call | flops 2147483648 | bytes 8388608 | tf_op jit(solution)/shard_map/product/pallas_call | solution.py:115
  25.8 0.1 collective-permute-start.5
  25.9 0.0 collective-permute-done.6.refs_2_
  25.9 0.6 collective-permute-start.7
  26.4 0.0 collective-permute-done.8.refs_4_
  26.5 0.1 collective-permute-start.9
  26.6 0.0 copy-start.3
  26.6 2.5 %collective-permute-start.2 = (bf16[1,64,1024]{2,1,0:T(8,128)(2,1)S(1)}, bf16[1,64,1024]{2,1,0:T(8,128)(2,1)S(1)}, u32[]{:S(2)}, u32[]{:S(2)}) collective-permute-start(bf16[1,64,1024]{2,1,0:T(8,128)(2,1)S(1)} %add_convert_fusion.7), channel_id=1, source_target_pairs={{0,3},{1,2},{2,1},{3,0},{4,7},{5,6},{6,5},{7,4},{8,11},{9,10},{10,... | collective-permute-start | bytes 393224 | tf_op jit(solution)/shard_map/ppermute | solution.py:188
  29.2 0.0 collective-permute-done.5.refs_1_
  29.2 7.5 %product.7 = (bf16[2,64,1024]{2,1,0:T(8,128)(2,1)S(1)}, bf16[2,64,1024]{2,1,0:T(8,128)(2,1)S(1)}, bf16[2,64,1024]{2,1,0:T(8,128)(2,1)S(1)}) custom-call(s32[4]{0:T(128)S(1)} %shift-right-arithmetic_xor_fusion.shard, bf16[2,2,32,1024]{3,2,1,0:T(8,128)(2,1)S(1)} %collective-permute-done.4.refs_0_, bf16[2,32,1024]{2,1,0:T(8,128)(2,1)S(1)} %collective-permute-done.5.refs_1_, ...), custom_call_target="tpu_custom_call" | custom-call | flops 2147483648 | bytes 8388608 | tf_op jit(solution)/shard_map/product/pallas_call | solution.py:115
  36.6 0.7 collective-permute-start.10
  37.4 1.3 %collective-permute-start.14 = (bf16[2,64,1024]{2,1,0:T(8,128)(2,1)S(1)}, bf16[2,64,1024]{2,1,0:T(8,128)(2,1)S(1)}, u32[]{:S(2)}, u32[]{:S(2)}) collective-permute-start(bf16[2,64,1024]{2,1,0:T(8,128)(2,1)S(1)} %get-tuple-element.24), channel_id=1, source_target_pairs={{0,1},{1,0},{2,3},{3,2},{4,5},{5,4},{6,7},{7,6},{8,9},{9,8},{10,11... | collective-permute-start | bytes 786440 | tf_op jit(solution)/shard_map/ppermute | solution.py:188
  38.7 0.7 collective-permute-start.18
  39.4 7.5 %product.6 = (bf16[2,64,1024]{2,1,0:T(8,128)(2,1)S(1)}, bf16[2,64,1024]{2,1,0:T(8,128)(2,1)S(1)}, bf16[2,64,1024]{2,1,0:T(8,128)(2,1)S(1)}) custom-call(s32[4]{0:T(128)S(1)} %shift-right-arithmetic_xor_fusion.shard, bf16[2,2,32,1024]{3,2,1,0:T(8,128)(2,1)S(1)} %collective-permute-done.4.refs_0_, bf16[2,32,1024]{2,1,0:T(8,128)(2,1)S(1)} %collective-permute-done.5.refs_1_, ...), custom_call_target="tpu_custom_call" | custom-call | flops 2147483648 | bytes 8388608 | tf_op jit(solution)/shard_map/product/pallas_call | solution.py:115
  46.9 0.0 collective-permute-done.2
  46.9 0.1 add_convert_fusion.6
  47.0 0.1 collective-permute-start.3
  47.1 2.1 %collective-permute-start.11 = (bf16[1,64,1024]{2,1,0:T(8,128)(2,1)S(1)}, bf16[1,64,1024]{2,1,0:T(8,128)(2,1)S(1)}, u32[]{:S(2)}, u32[]{:S(2)}) collective-permute-start(bf16[1,64,1024]{2,1,0:T(8,128)(2,1)S(1)} %add_convert_fusion.5), channel_id=1, source_target_pairs={{0,3},{1,2},{2,1},{3,0},{4,7},{5,6},{6,5},{7,4},{8,11},{9,10},{10,... | collective-permute-start | bytes 393224 | tf_op jit(solution)/shard_map/ppermute | solution.py:188
  49.2 2.2 %collective-permute-done.14 = bf16[2,64,1024]{2,1,0:T(8,128)(2,1)S(1)} collective-permute-done((bf16[2,64,1024]{2,1,0:T(8,128)(2,1)S(1)}, bf16[2,64,1024]{2,1,0:T(8,128)(2,1)S(1)}, u32[]{:S(2)}, u32[]{:S(2)}) %collective-permute-start.14) | collective-permute-done | bytes 262176 | tf_op jit(solution)/shard_map/ppermute | solution.py:188
  51.5 1.4 %collective-permute-start.15 = (bf16[1,64,1024]{2,1,0:T(8,128)(2,1)S(1)}, bf16[1,64,1024]{2,1,0:T(8,128)(2,1)S(1)}, u32[]{:S(2)}, u32[]{:S(2)}) collective-permute-start(bf16[1,64,1024]{2,1,0:T(8,128)(2,1)S(1)} %add_convert_fusion.3), channel_id=1, source_target_pairs={{0,3},{1,2},{2,1},{3,0},{4,7},{5,6},{6,5},{7,4},{8,11},{9,10},{10,... | collective-permute-start | bytes 393224 | tf_op jit(solution)/shard_map/ppermute | solution.py:188
  52.9 3.5 %collective-permute-done.18 = bf16[2,64,1024]{2,1,0:T(8,128)(2,1)S(1)} collective-permute-done((bf16[2,64,1024]{2,1,0:T(8,128)(2,1)S(1)}, bf16[2,64,1024]{2,1,0:T(8,128)(2,1)S(1)}, u32[]{:S(2)}, u32[]{:S(2)}) %collective-permute-start.18) | collective-permute-done | bytes 262176 | tf_op jit(solution)/shard_map/ppermute | solution.py:188
  56.5 1.3 %collective-permute-start.19 = (bf16[1,64,1024]{2,1,0:T(8,128)(2,1)S(1)}, bf16[1,64,1024]{2,1,0:T(8,128)(2,1)S(1)}, u32[]{:S(2)}, u32[]{:S(2)}) collective-permute-start(bf16[1,64,1024]{2,1,0:T(8,128)(2,1)S(1)} %add_convert_fusion.1), channel_id=1, source_target_pairs={{0,3},{1,2},{2,1},{3,0},{4,7},{5,6},{6,5},{7,4},{8,11},{9,10},{10,... | collective-permute-start | bytes 393224 | tf_op jit(solution)/shard_map/ppermute | solution.py:188
  57.8 2.9 %collective-permute-done.11 = bf16[1,64,1024]{2,1,0:T(8,128)(2,1)S(1)} collective-permute-done((bf16[1,64,1024]{2,1,0:T(8,128)(2,1)S(1)}, bf16[1,64,1024]{2,1,0:T(8,128)(2,1)S(1)}, u32[]{:S(2)}, u32[]{:S(2)}) %collective-permute-start.11) | collective-permute-done | bytes 131104 | tf_op jit(solution)/shard_map/ppermute | solution.py:188
  60.7 0.1 add_convert_fusion.4
  60.8 1.6 %collective-permute-start.12 = (bf16[2,32,1024]{2,1,0:T(8,128)(2,1)S(1)}, bf16[2,32,1024]{2,1,0:T(8,128)(2,1)S(1)}, u32[]{:S(2)}, u32[]{:S(2)}) collective-permute-start(bf16[2,32,1024]{2,1,0:T(8,128)(2,1)S(1)} %bitcast.23), channel_id=1, source_target_pairs={{0,8},{4,12},{8,0},{12,4},{16,24},{20,28},{24,16},{28,20},{1,9},{5... | collective-permute-start | bytes 393224 | tf_op jit(solution)/shard_map/ppermute | solution.py:185
  62.3 1.2 %collective-permute-done.15 = bf16[1,64,1024]{2,1,0:T(8,128)(2,1)S(1)} collective-permute-done((bf16[1,64,1024]{2,1,0:T(8,128)(2,1)S(1)}, bf16[1,64,1024]{2,1,0:T(8,128)(2,1)S(1)}, u32[]{:S(2)}, u32[]{:S(2)}) %collective-permute-start.15) | collective-permute-done | bytes 131104 | tf_op jit(solution)/shard_map/ppermute | solution.py:188
  63.5 0.1 add_convert_fusion.2
  63.6 1.6 %collective-permute-start.16 = (bf16[2,32,1024]{2,1,0:T(8,128)(2,1)S(1)}, bf16[2,32,1024]{2,1,0:T(8,128)(2,1)S(1)}, u32[]{:S(2)}, u32[]{:S(2)}) collective-permute-start(bf16[2,32,1024]{2,1,0:T(8,128)(2,1)S(1)} %bitcast.24), channel_id=1, source_target_pairs={{0,16},{4,20},{8,24},{12,28},{16,0},{20,4},{24,8},{28,12},{1,17},{... | collective-permute-start | bytes 393224 | tf_op jit(solution)/shard_map/ppermute | solution.py:185
  65.2 0.4 collective-permute-done.19
  65.6 0.1 add_convert_fusion
  65.6 2.5 %collective-permute-start.20 = (bf16[2,32,1024]{2,1,0:T(8,128)(2,1)S(1)}, bf16[2,32,1024]{2,1,0:T(8,128)(2,1)S(1)}, u32[]{:S(2)}, u32[]{:S(2)}) collective-permute-start(bf16[2,32,1024]{2,1,0:T(8,128)(2,1)S(1)} %bitcast.25), channel_id=1, source_target_pairs={{0,24},{4,28},{8,16},{12,20},{16,8},{20,12},{24,0},{28,4},{1,25},{... | collective-permute-start | bytes 393224 | tf_op jit(solution)/shard_map/ppermute | solution.py:185
  68.1 0.1 collective-permute-start.13
  68.2 1.8 %collective-permute-done.16.refs_4_ = bf16[2,32,1024]{2,1,0:T(8,128)(2,1)S(1)} collective-permute-done((bf16[2,32,1024]{2,1,0:T(8,128)(2,1)S(1)}, bf16[2,32,1024]{2,1,0:T(8,128)(2,1)S(1)}, u32[]{:S(2)}, u32[]{:S(2)}) %collective-permute-start.16) | collective-permute-done | bytes 131104 | tf_op jit(solution)/shard_map/ppermute | solution.py:185
  70.0 0.0 collective-permute-start.17
  70.0 1.5 %collective-permute-done.20.refs_6_ = bf16[2,32,1024]{2,1,0:T(8,128)(2,1)S(1)} collective-permute-done((bf16[2,32,1024]{2,1,0:T(8,128)(2,1)S(1)}, bf16[2,32,1024]{2,1,0:T(8,128)(2,1)S(1)}, u32[]{:S(2)}, u32[]{:S(2)}) %collective-permute-start.20) | collective-permute-done | bytes 131104 | tf_op jit(solution)/shard_map/ppermute | solution.py:185
  71.6 1.2 %collective-permute-done.21.refs_7_ = bf16[32,1024]{1,0:T(8,128)(2,1)S(1)} collective-permute-done((bf16[32,1024]{1,0:T(8,128)(2,1)S(1)}, bf16[32,1024]{1,0:T(8,128)(2,1)S(1)}, u32[]{:S(2)}, u32[]{:S(2)}) %collective-permute-start.21) | collective-permute-done | bytes 65568 | tf_op jit(solution)/shard_map/ppermute | solution.py:185
  72.8 2.5 %order.1 = bf16[32,8,1024]{2,1,0:T(8,128)(2,1)} custom-call(s32[8]{0:T(128)S(1)} %copy-done.3, bf16[2,32,1024]{2,1,0:T(8,128)(2,1)S(1)} %bitcast.20, bf16[32,1024]{1,0:T(8,128)(2,1)S(1)} %collective-permute-done.3.refs_1_, bf16[2,32,1024]{2,1,0:T(8,128)(2,1)S(1)} %collective-permute-done.12.refs_2_, bf16[32,1024]{1,0:T(8,128)(2,1)S(1)} %collective-permute-done.13.refs_3_, ...), custom_call_target="tpu_custom_call" | custom-call | tf_op jit(solution)/shard_map/order/pallas_call | solution.py:160
  (28 shorter events, 0.2 us)
Async XLA Ops:
  0.0 0.9 %copy-start = (bf16[32,4,1024]{2,1,0:T(4,128)(2,1)S(1)}, bf16[32,4,1024]{2,1,0:T(4,128)(2,1)}, u32[]{:S(2)}) copy-start(bf16[32,4,1024]{2,1,0:T(4,128)(2,1)} %amps.1) | copy-start | bytes 786436
  1.0 0.7 copy-start.1
  1.6 0.7 copy-start.2
  2.3 0.7 copy-start.4
  4.3 4.6 %collective-permute-start = (bf16[2,32,1024]{2,1,0:T(8,128)(2,1)S(1)}, bf16[2,32,1024]{2,1,0:T(8,128)(2,1)S(1)}, u32[]{:S(2)}, u32[]{:S(2)}) collective-permute-start(bf16[2,32,1024]{2,1,0:T(8,128)(2,1)S(1)} %get-tuple-element.17), channel_id=1, source_target_pairs={{0,4},{4,0},{8,12},{12,8},{16,20},{20,16},{24,28},{28,24},{1,5},{5... | collective-permute-start | bytes 393224 | tf_op jit(solution)/shard_map/ppermute | solution.py:185
  4.8 20.9 %collective-permute-start.4 = (bf16[2,2,32,1024]{3,2,1,0:T(8,128)(2,1)S(1)}, bf16[2,2,32,1024]{3,2,1,0:T(8,128)(2,1)S(1)}, u32[]{:S(2)}, u32[]{:S(2)}) collective-permute-start(bf16[2,2,32,1024]{3,2,1,0:T(8,128)(2,1)S(1)} %get-tuple-element.18), channel_id=1, source_target_pairs={{0,8},{4,12},{8,0},{12,4},{16,24},{20,28},{24,16},{28,20},{1,9},{5... | collective-permute-start | bytes 786440 | tf_op jit(solution)/shard_map/ppermute | solution.py:185
  7.4 18.5 %collective-permute-start.6 = (bf16[2,2,32,1024]{3,2,1,0:T(8,128)(2,1)S(1)}, bf16[2,2,32,1024]{3,2,1,0:T(8,128)(2,1)S(1)}, u32[]{:S(2)}, u32[]{:S(2)}) collective-permute-start(bf16[2,2,32,1024]{3,2,1,0:T(8,128)(2,1)S(1)} %get-tuple-element.19), channel_id=1, source_target_pairs={{0,16},{4,20},{8,24},{12,28},{16,0},{20,4},{24,8},{28,12},{1,17},{... | collective-permute-start | bytes 786440 | tf_op jit(solution)/shard_map/ppermute | solution.py:185
  8.9 17.5 %collective-permute-start.8 = (bf16[2,2,32,1024]{3,2,1,0:T(8,128)(2,1)S(1)}, bf16[2,2,32,1024]{3,2,1,0:T(8,128)(2,1)S(1)}, u32[]{:S(2)}, u32[]{:S(2)}) collective-permute-start(bf16[2,2,32,1024]{3,2,1,0:T(8,128)(2,1)S(1)} %get-tuple-element.20), channel_id=1, source_target_pairs={{0,24},{4,28},{8,16},{12,20},{16,8},{20,12},{24,0},{28,4},{1,25},{... | collective-permute-start | bytes 786440 | tf_op jit(solution)/shard_map/ppermute | solution.py:185
  16.3 10.2 %collective-permute-start.1 = (bf16[2,64,1024]{2,1,0:T(8,128)(2,1)S(1)}, bf16[2,64,1024]{2,1,0:T(8,128)(2,1)S(1)}, u32[]{:S(2)}, u32[]{:S(2)}) collective-permute-start(bf16[2,64,1024]{2,1,0:T(8,128)(2,1)S(1)} %product.5), channel_id=1, source_target_pairs={{0,1},{1,0},{2,3},{3,2},{4,5},{5,4},{6,7},{7,6},{8,9},{9,8},{10,11... | collective-permute-start | bytes 786440 | tf_op jit(solution)/shard_map/ppermute | solution.py:188
  25.8 3.4 %collective-permute-start.5 = (bf16[2,32,1024]{2,1,0:T(8,128)(2,1)S(1)}, bf16[2,32,1024]{2,1,0:T(8,128)(2,1)S(1)}, u32[]{:S(2)}, u32[]{:S(2)}) collective-permute-start(bf16[2,32,1024]{2,1,0:T(8,128)(2,1)S(1)} %slice_bitcast_fusion.2), channel_id=1, source_target_pairs={{0,4},{4,0},{8,12},{12,8},{16,20},{20,16},{24,28},{28,24},{1,5},{5... | collective-permute-start | bytes 393224 | tf_op jit(solution)/shard_map/ppermute | solution.py:185
  25.9 3.3 %collective-permute-start.7 = (bf16[2,32,1024]{2,1,0:T(8,128)(2,1)S(1)}, bf16[2,32,1024]{2,1,0:T(8,128)(2,1)S(1)}, u32[]{:S(2)}, u32[]{:S(2)}) collective-permute-start(bf16[2,32,1024]{2,1,0:T(8,128)(2,1)S(1)} %slice_bitcast_fusion.1), channel_id=1, source_target_pairs={{0,4},{4,0},{8,12},{12,8},{16,20},{20,16},{24,28},{28,24},{1,5},{5... | collective-permute-start | bytes 393224 | tf_op jit(solution)/shard_map/ppermute | solution.py:185
  26.5 2.7 %collective-permute-start.9 = (bf16[2,32,1024]{2,1,0:T(8,128)(2,1)S(1)}, bf16[2,32,1024]{2,1,0:T(8,128)(2,1)S(1)}, u32[]{:S(2)}, u32[]{:S(2)}) collective-permute-start(bf16[2,32,1024]{2,1,0:T(8,128)(2,1)S(1)} %slice_bitcast_fusion), channel_id=1, source_target_pairs={{0,4},{4,0},{8,12},{12,8},{16,20},{20,16},{24,28},{28,24},{1,5},{5... | collective-permute-start | bytes 393224 | tf_op jit(solution)/shard_map/ppermute | solution.py:185
  26.6 46.2 %copy-start.3 = (s32[8]{0:T(128)S(1)}, s32[8]{0:T(128)}, u32[]{:S(2)}) copy-start(s32[8]{0:T(128)} %q_owner.3) | copy-start | bytes 100
  26.6 20.3 %collective-permute-start.2 = (bf16[1,64,1024]{2,1,0:T(8,128)(2,1)S(1)}, bf16[1,64,1024]{2,1,0:T(8,128)(2,1)S(1)}, u32[]{:S(2)}, u32[]{:S(2)}) collective-permute-start(bf16[1,64,1024]{2,1,0:T(8,128)(2,1)S(1)} %add_convert_fusion.7), channel_id=1, source_target_pairs={{0,3},{1,2},{2,1},{3,0},{4,7},{5,6},{6,5},{7,4},{8,11},{9,10},{10,... | collective-permute-start | bytes 393224 | tf_op jit(solution)/shard_map/ppermute | solution.py:188
  36.6 10.4 %collective-permute-start.10 = (bf16[2,64,1024]{2,1,0:T(8,128)(2,1)S(1)}, bf16[2,64,1024]{2,1,0:T(8,128)(2,1)S(1)}, u32[]{:S(2)}, u32[]{:S(2)}) collective-permute-start(bf16[2,64,1024]{2,1,0:T(8,128)(2,1)S(1)} %get-tuple-element.22), channel_id=1, source_target_pairs={{0,1},{1,0},{2,3},{3,2},{4,5},{5,4},{6,7},{7,6},{8,9},{9,8},{10,11... | collective-permute-start | bytes 786440 | tf_op jit(solution)/shard_map/ppermute | solution.py:188
  37.4 14.1 %collective-permute-start.14 = (bf16[2,64,1024]{2,1,0:T(8,128)(2,1)S(1)}, bf16[2,64,1024]{2,1,0:T(8,128)(2,1)S(1)}, u32[]{:S(2)}, u32[]{:S(2)}) collective-permute-start(bf16[2,64,1024]{2,1,0:T(8,128)(2,1)S(1)} %get-tuple-element.24), channel_id=1, source_target_pairs={{0,1},{1,0},{2,3},{3,2},{4,5},{5,4},{6,7},{7,6},{8,9},{9,8},{10,11... | collective-permute-start | bytes 786440 | tf_op jit(solution)/shard_map/ppermute | solution.py:188
  38.7 17.7 %collective-permute-start.18 = (bf16[2,64,1024]{2,1,0:T(8,128)(2,1)S(1)}, bf16[2,64,1024]{2,1,0:T(8,128)(2,1)S(1)}, u32[]{:S(2)}, u32[]{:S(2)}) collective-permute-start(bf16[2,64,1024]{2,1,0:T(8,128)(2,1)S(1)} %get-tuple-element.26), channel_id=1, source_target_pairs={{0,1},{1,0},{2,3},{3,2},{4,5},{5,4},{6,7},{7,6},{8,9},{9,8},{10,11... | collective-permute-start | bytes 786440 | tf_op jit(solution)/shard_map/ppermute | solution.py:188
  47.0 24.6 %collective-permute-start.3 = (bf16[32,1024]{1,0:T(8,128)(2,1)S(1)}, bf16[32,1024]{1,0:T(8,128)(2,1)S(1)}, u32[]{:S(2)}, u32[]{:S(2)}) collective-permute-start(bf16[32,1024]{1,0:T(8,128)(2,1)S(1)} %slice_bitcast_fusion.6), channel_id=1, source_target_pairs={{0,4},{4,0},{8,12},{12,8},{16,20},{20,16},{24,28},{28,24},{1,5},{5... | collective-permute-start | bytes 196616 | tf_op jit(solution)/shard_map/ppermute | solution.py:185
  47.1 13.6 %collective-permute-start.11 = (bf16[1,64,1024]{2,1,0:T(8,128)(2,1)S(1)}, bf16[1,64,1024]{2,1,0:T(8,128)(2,1)S(1)}, u32[]{:S(2)}, u32[]{:S(2)}) collective-permute-start(bf16[1,64,1024]{2,1,0:T(8,128)(2,1)S(1)} %add_convert_fusion.5), channel_id=1, source_target_pairs={{0,3},{1,2},{2,1},{3,0},{4,7},{5,6},{6,5},{7,4},{8,11},{9,10},{10,... | collective-permute-start | bytes 393224 | tf_op jit(solution)/shard_map/ppermute | solution.py:188
  51.5 12.0 %collective-permute-start.15 = (bf16[1,64,1024]{2,1,0:T(8,128)(2,1)S(1)}, bf16[1,64,1024]{2,1,0:T(8,128)(2,1)S(1)}, u32[]{:S(2)}, u32[]{:S(2)}) collective-permute-start(bf16[1,64,1024]{2,1,0:T(8,128)(2,1)S(1)} %add_convert_fusion.3), channel_id=1, source_target_pairs={{0,3},{1,2},{2,1},{3,0},{4,7},{5,6},{6,5},{7,4},{8,11},{9,10},{10,... | collective-permute-start | bytes 393224 | tf_op jit(solution)/shard_map/ppermute | solution.py:188
  56.5 9.1 %collective-permute-start.19 = (bf16[1,64,1024]{2,1,0:T(8,128)(2,1)S(1)}, bf16[1,64,1024]{2,1,0:T(8,128)(2,1)S(1)}, u32[]{:S(2)}, u32[]{:S(2)}) collective-permute-start(bf16[1,64,1024]{2,1,0:T(8,128)(2,1)S(1)} %add_convert_fusion.1), channel_id=1, source_target_pairs={{0,3},{1,2},{2,1},{3,0},{4,7},{5,6},{6,5},{7,4},{8,11},{9,10},{10,... | collective-permute-start | bytes 393224 | tf_op jit(solution)/shard_map/ppermute | solution.py:188
  60.8 7.3 %collective-permute-start.12 = (bf16[2,32,1024]{2,1,0:T(8,128)(2,1)S(1)}, bf16[2,32,1024]{2,1,0:T(8,128)(2,1)S(1)}, u32[]{:S(2)}, u32[]{:S(2)}) collective-permute-start(bf16[2,32,1024]{2,1,0:T(8,128)(2,1)S(1)} %bitcast.23), channel_id=1, source_target_pairs={{0,8},{4,12},{8,0},{12,4},{16,24},{20,28},{24,16},{28,20},{1,9},{5... | collective-permute-start | bytes 393224 | tf_op jit(solution)/shard_map/ppermute | solution.py:185
  63.6 6.4 %collective-permute-start.16 = (bf16[2,32,1024]{2,1,0:T(8,128)(2,1)S(1)}, bf16[2,32,1024]{2,1,0:T(8,128)(2,1)S(1)}, u32[]{:S(2)}, u32[]{:S(2)}) collective-permute-start(bf16[2,32,1024]{2,1,0:T(8,128)(2,1)S(1)} %bitcast.24), channel_id=1, source_target_pairs={{0,16},{4,20},{8,24},{12,28},{16,0},{20,4},{24,8},{28,12},{1,17},{... | collective-permute-start | bytes 393224 | tf_op jit(solution)/shard_map/ppermute | solution.py:185
  65.6 5.9 %collective-permute-start.20 = (bf16[2,32,1024]{2,1,0:T(8,128)(2,1)S(1)}, bf16[2,32,1024]{2,1,0:T(8,128)(2,1)S(1)}, u32[]{:S(2)}, u32[]{:S(2)}) collective-permute-start(bf16[2,32,1024]{2,1,0:T(8,128)(2,1)S(1)} %bitcast.25), channel_id=1, source_target_pairs={{0,24},{4,28},{8,16},{12,20},{16,8},{20,12},{24,0},{28,4},{1,25},{... | collective-permute-start | bytes 393224 | tf_op jit(solution)/shard_map/ppermute | solution.py:185
  68.1 3.4 %collective-permute-start.13 = (bf16[32,1024]{1,0:T(8,128)(2,1)S(1)}, bf16[32,1024]{1,0:T(8,128)(2,1)S(1)}, u32[]{:S(2)}, u32[]{:S(2)}) collective-permute-start(bf16[32,1024]{1,0:T(8,128)(2,1)S(1)} %slice_bitcast_fusion.5), channel_id=1, source_target_pairs={{0,4},{4,0},{8,12},{12,8},{16,20},{20,16},{24,28},{28,24},{1,5},{5... | collective-permute-start | bytes 196616 | tf_op jit(solution)/shard_map/ppermute | solution.py:185
  70.0 1.6 %collective-permute-start.17 = (bf16[32,1024]{1,0:T(8,128)(2,1)S(1)}, bf16[32,1024]{1,0:T(8,128)(2,1)S(1)}, u32[]{:S(2)}, u32[]{:S(2)}) collective-permute-start(bf16[32,1024]{1,0:T(8,128)(2,1)S(1)} %slice_bitcast_fusion.4), channel_id=1, source_target_pairs={{0,4},{4,0},{8,12},{12,8},{16,20},{20,16},{24,28},{28,24},{1,5},{5... | collective-permute-start | bytes 196616 | tf_op jit(solution)/shard_map/ppermute | solution.py:185
  71.6 1.3 %collective-permute-start.21 = (bf16[32,1024]{1,0:T(8,128)(2,1)S(1)}, bf16[32,1024]{1,0:T(8,128)(2,1)S(1)}, u32[]{:S(2)}, u32[]{:S(2)}) collective-permute-start(bf16[32,1024]{1,0:T(8,128)(2,1)S(1)} %slice_bitcast_fusion.3), channel_id=1, source_target_pairs={{0,4},{4,0},{8,12},{12,8},{16,20},{20,16},{24,28},{28,24},{1,5},{5... | collective-permute-start | bytes 196616 | tf_op jit(solution)/shard_map/ppermute | solution.py:185
where the time goes:
time: 76.5 us; the launch traced here: 75.3 us
  Pallas kernels  33.4 us (44%)
  starting transfers between devices  23.4 us (31%)
  waiting for transfers between devices  14.8 us (19%)
  local copies, waits for them, and re-layouts  3.02 us (4%)
    pallas_call x4, Pallas kernels, product(): pl.pallas_call(functools.partial(product_kernel, halves, chunks, rows, or...  29.6 us
    ppermute x8, starting transfers between devices, swap_line(): lax.ppermute(value, 'narrow', [(n, n ^ mask) for n in range(devices)])  12.3 us
    ppermute x14, starting transfers between devices, swap(): return lax.ppermute(value, 'wide', [(w, w ^ j) for w in range(peers)])  11.1 us
    ppermute x8, waiting for transfers between devices, swap_line(): lax.ppermute(value, 'narrow', [(n, n ^ mask) for n in range(devices)])  10.3 us
    ppermute x14, waiting for transfers between devices, swap(): return lax.ppermute(value, 'wide', [(w, w ^ j) for w in range(peers)])  4.56 us
    unnamed x10, local copies, waits for them, and re-layouts  2.97 us
    pallas_call x1, Pallas kernels, order(): pl.pallas_call(functools.partial(order_kernel, peers, [h for _, h in shar...  2.49 us
  transfers between devices with their start and end apart: 22, of which 8 were waited for; matrix products, arithmetic and copies ran while one was open for 1% of the time, Pallas kernels for 39%

commit v1 on v0

--- a/solution.py
+++ b/solution.py
@@ -12,9 +12,17 @@
 LIMIT = 48 << 20
 
 
-def pick_kernel(peers, amp_tiles, cd_tiles, q_owner, amps, *rest):
-    own, mate, *outs = rest[: peers // 2 + 1]
-    held, slots = rest[peers // 2 + 1 :]
+def pick_kernel(peers, *refs):
+    given, own, mate, *outs = refs[:4], *refs[4 : peers // 2 + 5]
+    amp_tiles, cd_tiles, q_owner, amps, held, slots, sems = refs[peers // 2 + 5 :]
+    copies = [
+        pltpu.make_async_copy(source, target, sems.at[i])
+        for i, (source, target) in enumerate(zip(given, (amp_tiles, cd_tiles, q_owner, amps)))
+    ]
+    for copy in copies:
+        copy.start()
+    for copy in copies[:3]:
+        copy.wait()
     width = amps.shape[1]
     wants = cd_tiles.shape[0]
     me = lax.axis_index("wide")
@@ -29,6 +37,7 @@
         return carry
 
     lax.fori_loop(0, peers, look, 0)
+    copies[3].wait()
     for t in range(width):
         held[t] = amps[:, t, :]
     held[width] = jnp.zeros_like(held[width])
@@ -41,19 +50,23 @@
 def pick(amplitudes, amp_tiles, cd_tiles, q_owner):
     rows, width, depth = amplitudes.shape
     peers, wants = cd_tiles.shape
-    smem = pl.BlockSpec(memory_space=pltpu.SMEM)
     vmem = pl.BlockSpec(memory_space=pltpu.VMEM)
     return pl.pallas_call(
         functools.partial(pick_kernel, peers),
         out_shape=[jax.ShapeDtypeStruct((wants, rows, depth), jnp.bfloat16)] * 2
         + [jax.ShapeDtypeStruct((2, wants, rows, depth), jnp.bfloat16)] * (peers // 2 - 1),
-        in_specs=[smem, smem, smem, vmem],
+        in_specs=[pl.BlockSpec(memory_space=pltpu.HBM)] * 4,
         out_specs=[vmem] * (peers // 2 + 1),
         scratch_shapes=[
+            pltpu.SMEM((width, amp_tiles.shape[0]), jnp.int32),
+            pltpu.SMEM((wants, peers), jnp.int32),
+            pltpu.SMEM((peers,), jnp.int32),
+            pltpu.VMEM(amplitudes.shape, jnp.bfloat16),
             pltpu.VMEM((width + 1, rows, depth), jnp.bfloat16),
             pltpu.SMEM((peers, wants), jnp.int32),
+            pltpu.SemaphoreType.DMA((4,)),
         ],
-        compiler_params=pltpu.CompilerParams(vmem_limit_bytes=LIMIT),
+        compiler_params=pltpu.CompilerParams(vmem_limit_bytes=60 << 20),
         name="pick",
     )(amp_tiles.T, cd_tiles.T, q_owner, amplitudes)
 
@@ -63,7 +76,7 @@
     picked = [refs.pop(0) for _ in range(len(halves))]
     ints = refs.pop(0)
     outs = [refs.pop(0) for _ in range(chunks)]
-    buffer, turned, padded, sems = refs
+    buffer, left, sems = refs
     shares, wants, share, depth = buffer.shape
     pieces = sems.shape[2]
     piece = share // pieces
@@ -79,11 +92,9 @@
             for k in range(wants):
                 copy(s, k, p).start()
 
-    padded[...] = jnp.zeros_like(padded)
     for k in range(wants):
         for i, (ref, half) in enumerate(zip(picked, halves)):
-            padded[i * rows : (i + 1) * rows, :] = ref[k] if half is None else ref[half, k]
-        turned[k] = padded[...].T
+            left[k, i * rows : (i + 1) * rows, :] = ref[k] if half is None else ref[half, k]
 
     each = len(halves) * rows // chunks
     part = min(PART, share)
@@ -95,9 +106,11 @@
                     copy(s, k, p).wait()
             total = None
             for k in range(wants):
-                term = jnp.dot(buffer[s, k, at, :], turned[k], preferred_element_type=jnp.float32)
+                term = lax.dot_general(
+                    left[k], buffer[s, k, at, :], (((1,), (1,)), ((), ())), preferred_element_type=jnp.float32
+                )
                 total = term if total is None else total + term
-            total = total.T.astype(jnp.bfloat16)
+            total = total.astype(jnp.bfloat16)
             for c in range(chunks):
                 outs[c][s, :, at] = total[c * each : (c + 1) * each]
 
@@ -107,7 +120,6 @@
     _, wants, pairs, depth = ints.shape
     share = pairs // shard.shape[0]
     count = len(picked)
-    lanes = -(-count * rows // 128) * 128
     each = count * rows // chunks
     shares = len(order)
     pieces = max(1, share // PIECE)
@@ -115,12 +127,11 @@
     return pl.pallas_call(
         functools.partial(product_kernel, halves, chunks, rows, order),
         out_shape=[jax.ShapeDtypeStruct((shares, each, share), jnp.bfloat16)] * chunks,
-        in_specs=[pl.BlockSpec(memory_space=pltpu.SMEM)] + [vmem] * count + [pl.BlockSpec(memory_space=pl.ANY)],
+        in_specs=[pl.BlockSpec(memory_space=pltpu.SMEM)] + [vmem] * count + [pl.BlockSpec(memory_space=pltpu.HBM)],
         out_specs=[vmem] * chunks,
         scratch_shapes=[
             pltpu.VMEM((shares, wants, share, depth), jnp.bfloat16),
-            pltpu.VMEM((wants, depth, lanes), jnp.bfloat16),
-            pltpu.VMEM((lanes, depth), jnp.bfloat16),
+            pltpu.VMEM((wants, count * rows, depth), jnp.bfloat16),
             pltpu.SemaphoreType.DMA((shares, wants, pieces)),
         ],
         compiler_params=pltpu.CompilerParams(vmem_limit_bytes=LIMIT),
@@ -137,35 +148,26 @@
     return sum(t.astype(jnp.float32) for t in terms).astype(jnp.bfloat16)
 
 
-def order_kernel(peers, halves, q_owner, *refs):
-    shares, out, held = refs[:peers], refs[peers], refs[peers + 1]
-    me = lax.axis_index("wide")
-
-    def tile_of(j):
-        def look(q, found):
-            return jnp.where(q_owner[q] == me ^ j, q, found)
-
-        return lax.fori_loop(0, peers, look, jnp.int32(0))
-
-    for j in range(peers):
-        held[tile_of(j)] = shares[j][...] if halves[j] is None else shares[j][halves[j]]
-    for q in range(peers):
-        out[:, q, :] = held[q]
-
-
-def order(q_owner, shares, rows):
-    peers = len(shares)
-    share = shares[0][0].shape[-1]
+def order_kernel(halves, place, *refs):
+    shares, out, held = refs[: len(halves)], refs[-2], refs[-1]
+    rows = held.shape[0] // len(halves)
+    for j, (share, half) in enumerate(zip(shares, halves)):
+        held[j * rows : (j + 1) * rows, :] = share[...] if half is None else share[half]
+    out[...] = jnp.dot(place[...], held[...], preferred_element_type=jnp.float32).astype(jnp.bfloat16)
+
+
+def order(place, shares):
+    size, share = place.shape[0], shares[0][0].shape[-1]
     vmem = pl.BlockSpec(memory_space=pltpu.VMEM)
     return pl.pallas_call(
-        functools.partial(order_kernel, peers, [h for _, h in shares]),
-        out_shape=jax.ShapeDtypeStruct((rows, peers, share), jnp.bfloat16),
-        in_specs=[pl.BlockSpec(memory_space=pltpu.SMEM)] + [vmem] * peers,
+        functools.partial(order_kernel, [h for _, h in shares]),
+        out_shape=jax.ShapeDtypeStruct((size, share), jnp.bfloat16),
+        in_specs=[vmem] * (1 + len(shares)),
         out_specs=vmem,
-        scratch_shapes=[pltpu.VMEM((peers, rows, share), jnp.bfloat16)],
+        scratch_shapes=[pltpu.VMEM((size, share), jnp.bfloat16)],
         compiler_params=pltpu.CompilerParams(vmem_limit_bytes=LIMIT),
         name="order",
-    )(q_owner, *[s for s, _ in shares])
+    )(place, *[s for s, _ in shares])
 
 
 def on_device(amplitudes, amp_tiles, integrals, cd_tiles, q_owner):
@@ -194,9 +196,15 @@
     first = [(mine, None), (mate, None)]
     rest = [pair for g in range(1, peers // 2) for pair in ((arrived[g], 0), (handed[g], None))]
 
-    def totals(group, chunks):
+    wide = jnp.arange(peers * rows, dtype=jnp.int32)
+    source = (q_owner ^ lax.axis_index("wide"))[None, :] * rows + jnp.arange(rows, dtype=jnp.int32)[:, None]
+    place = (source.reshape(-1, 1) == wide[None, :]).astype(jnp.bfloat16)
+
+    def totals(group, chunks, beside=None):
         away = product(shard, odd, group, integrals, rows, chunks)
         keep = product(shard, even, group, integrals, rows, chunks)
+        if beside is not None:
+            keep, beside = lax.optimization_barrier((keep, beside))
         results = []
         for c in range(chunks):
             terms = {2 * i: [keep[c][i]] for i in range(devices // 2)}
@@ -212,14 +220,14 @@
                 names = [r for r in sorted(terms) if r >> step & 1]
                 message = jnp.stack([add(*terms.pop(r)) for r in names])
             results.append(add(*terms[0]).reshape(2, rows, -1))
-        return results
-
-    own, = totals(first, 1)
+        return results, beside
+
+    (own,), place = totals(first, 1, place)
     shares = [(own, 0), (swap(own[1], 1), None)]
-    for g, total in enumerate(totals(rest, peers // 2 - 1), 1):
+    for g, total in enumerate(totals(rest, peers // 2 - 1)[0], 1):
         got = swap(total, 2 * g)
         shares += [(got, 0), (swap(got[1], 1), None)]
-    return order(q_owner, shares, rows)
+    return order(place, shares).reshape(rows, peers, -1)
 
 
 def solution(mesh):

time: 76.5 us -> 76.5 us (level); the launches traced: 75.3 us -> 76.3 us
  waiting for transfers between devices: 14.8 us -> 25.1 us
  Pallas kernels: 33.4 us -> 25.3 us
  local copies, waits for them, and re-layouts: 3.02 us -> 1.04 us
    pallas_call x4, Pallas kernels: 29.6 us -> 21.7 us  [product(): pl.pallas_call(functools.partial(product_kernel, halves, chunks, rows, or...]
    ppermute x8, waiting for transfers between devices: 10.3 us -> 17.2 us  [swap_line(): lax.ppermute(value, 'narrow', [(n, n ^ mask) for n in range(devices)])]
    ppermute x14, waiting for transfers between devices: 4.56 us -> 7.91 us  [swap(): return lax.ppermute(value, 'wide', [(w, w ^ j) for w in range(peers)])]
    unnamed x10 -> x2, local copies, waits for them, and re-layouts: 2.97 us -> 0.9 us
    ppermute x8, starting transfers between devices: 12.3 us -> 13.7 us  [swap_line(): lax.ppermute(value, 'narrow', [(n, n ^ mask) for n in range(devices)])]
    ppermute x14, starting transfers between devices: 11.1 us -> 9.71 us  [swap(): return lax.ppermute(value, 'wide', [(w, w ^ j) for w in range(peers)])]
    pallas_call x1, Pallas kernels: 2.49 us -> 1.1 us  [order(): pl.pallas_call(functools.partial(order_kernel, [h for _, h in shares]), o...]
    pallas_call x1, Pallas kernels: 1.35 us -> 2.5 us  [pick(): pl.pallas_call(functools.partial(pick_kernel, peers), out_shape=[jax.Shap...]
  transfers between devices with their start and end apart: 22 -> 22, of which waited for: 8 -> 9; matrix products, arithmetic and copies ran while one was open for 1% -> 2% of each run, Pallas kernels for 39% -> 28%
where the time goes in v1:
time: 76.5 us; the launch traced here: 76.3 us
  Pallas kernels  25.3 us (33%)
  waiting for transfers between devices  25.1 us (33%)
  starting transfers between devices  23.4 us (31%)
  other arithmetic  1.13 us (1%)
  local copies, waits for them, and re-layouts  1.04 us (1%)
    pallas_call x4, Pallas kernels, product(): pl.pallas_call(functools.partial(product_kernel, halves, chunks, rows, or...  21.7 us
    ppermute x8, waiting for transfers between devices, swap_line(): lax.ppermute(value, 'narrow', [(n, n ^ mask) for n in range(devices)])  17.2 us
    ppermute x8, starting transfers between devices, swap_line(): lax.ppermute(value, 'narrow', [(n, n ^ mask) for n in range(devices)])  13.7 us
    ppermute x14, starting transfers between devices, swap(): return lax.ppermute(value, 'wide', [(w, w ^ j) for w in range(peers)])  9.71 us
    ppermute x14, waiting for transfers between devices, swap(): return lax.ppermute(value, 'wide', [(w, w ^ j) for w in range(peers)])  7.91 us
    pallas_call x1, Pallas kernels, pick(): pl.pallas_call(functools.partial(pick_kernel, peers), out_shape=[jax.Shap...  2.5 us
  transfers between devices with their start and end apart: 22, of which 9 were waited for; matrix products, arithmetic and copies ran while one was open for 2% of the time, Pallas kernels for 28%

profile of v1, /device:TPU:0, one launch (start us, length us, event | category | flops | bytes accessed | tf_op | source)
XLA Modules:
  0.0 76.3 jit_solution(4321970710337058595)
XLA Ops:
  0.0 2.5 %pick.1 = (bf16[2,32,1024]{2,1,0:T(8,128)(2,1)}, bf16[2,32,1024]{2,1,0:T(8,128)(2,1)}, bf16[2,2,32,1024]{3,2,1,0:T(8,128)(2,1)}, bf16[2,2,32,1024]{3,2,1,0:T(8,128)(2,1)}, bf16[2,2,32,1024]{3,2,1,0:T(8,128)(2,1)}) custom-call(s32[4,8]{1,0:T(4,128)} %bitcast.25, s32[2,8]{1,0:T(2,128)} %bitcast.26, s32[8]{0:T(128)} %refs_2_.3, bf16[32,4,1024]{2,1,0:T(4,128)(2,1)} %refs_3_.1), custom_call_target="tpu_custom_call" | custom-call | tf_op jit(solution)/shard_map/pick/pallas_call | solution.py:54
  2.5 3.0 %collective-permute-start.4 = (bf16[2,2,32,1024]{3,2,1,0:T(8,128)(2,1)}, bf16[2,2,32,1024]{3,2,1,0:T(8,128)(2,1)S(1)}, u32[]{:S(2)}, u32[]{:S(2)}) collective-permute-start(bf16[2,2,32,1024]{3,2,1,0:T(8,128)(2,1)} %get-tuple-element.22), channel_id=1, source_target_pairs={{0,8},{4,12},{8,0},{12,4},{16,24},{20,28},{24,16},{28,20},{1,9},{5... | collective-permute-start | bytes 786440 | tf_op jit(solution)/shard_map/ppermute | solution.py:187
  5.5 1.5 %collective-permute-start.6 = (bf16[2,2,32,1024]{3,2,1,0:T(8,128)(2,1)}, bf16[2,2,32,1024]{3,2,1,0:T(8,128)(2,1)S(1)}, u32[]{:S(2)}, u32[]{:S(2)}) collective-permute-start(bf16[2,2,32,1024]{3,2,1,0:T(8,128)(2,1)} %get-tuple-element.23), channel_id=1, source_target_pairs={{0,16},{4,20},{8,24},{12,28},{16,0},{20,4},{24,8},{28,12},{1,17},{... | collective-permute-start | bytes 786440 | tf_op jit(solution)/shard_map/ppermute | solution.py:187
  7.0 0.0 collective-permute-start.8
  7.1 0.7 xor_multiply_fusion
  7.7 0.1 add.81
  7.8 0.1 fusion.place
  7.9 0.7 collective-permute-done.refs_1_
  8.6 0.9 %copy-done = bf16[2,32,1024]{2,1,0:T(8,128)(2,1)S(1)} copy-done((bf16[2,32,1024]{2,1,0:T(8,128)(2,1)S(1)}, bf16[2,32,1024]{2,1,0:T(8,128)(2,1)}, u32[]{:S(2)}) %copy-start) | copy-done | bytes 131096
  9.5 5.3 %product.5 = bf16[2,64,1024]{2,1,0:T(8,128)(2,1)S(1)} custom-call(s32[4]{0:T(128)S(1)} %shift-right-arithmetic_xor_fusion.shard, bf16[2,32,1024]{2,1,0:T(8,128)(2,1)S(1)} %copy-done, bf16[2,32,1024]{2,1,0:T(8,128)(2,1)S(1)} %collective-permute-done.refs_1_, bf16[1,2,4096,1024]{3,2,1,0:T(8,128)(2,1)} %refs_6_.3), custom_call_target="tpu_custom_call" | custom-call | flops 2147483648 | bytes 8388608 | tf_op jit(solution)/shard_map/product/pallas_call | solution.py:127
  14.8 2.1 %collective-permute-start.1 = (bf16[2,64,1024]{2,1,0:T(8,128)(2,1)S(1)}, bf16[2,64,1024]{2,1,0:T(8,128)(2,1)S(1)}, u32[]{:S(2)}, u32[]{:S(2)}) collective-permute-start(bf16[2,64,1024]{2,1,0:T(8,128)(2,1)S(1)} %product.5), channel_id=1, source_target_pairs={{0,1},{1,0},{2,3},{3,2},{4,5},{5,4},{6,7},{7,6},{8,9},{9,8},{10,11... | collective-permute-start | bytes 786440 | tf_op jit(solution)/shard_map/ppermute | solution.py:190
  16.9 0.1 collective-permute-start.5
  17.0 2.1 %collective-permute-done.6.refs_2_ = bf16[2,2,32,1024]{3,2,1,0:T(8,128)(2,1)S(1)} collective-permute-done((bf16[2,2,32,1024]{3,2,1,0:T(8,128)(2,1)}, bf16[2,2,32,1024]{3,2,1,0:T(8,128)(2,1)S(1)}, u32[]{:S(2)}, u32[]{:S(2)}) %collective-permute-start.6) | collective-permute-done | bytes 262176 | tf_op jit(solution)/shard_map/ppermute | solution.py:187
  19.1 0.1 collective-permute-start.7
  19.2 0.0 collective-permute-done.8.refs_4_
  19.2 0.6 collective-permute-start.9
  19.8 5.3 %product.4 = bf16[2,64,1024]{2,1,0:T(8,128)(2,1)S(1)} custom-call(s32[4]{0:T(128)S(1)} %shift-right-arithmetic_xor_fusion.shard, bf16[2,32,1024]{2,1,0:T(8,128)(2,1)S(1)} %copy-done, bf16[2,32,1024]{2,1,0:T(8,128)(2,1)S(1)} %collective-permute-done.refs_1_, bf16[1,2,4096,1024]{3,2,1,0:T(8,128)(2,1)} %refs_6_.3), custom_call_target="tpu_custom_call" | custom-call | flops 2147483648 | bytes 8388608 | tf_op jit(solution)/shard_map/product/pallas_call | solution.py:127
  25.0 0.0 collective-permute-done.5.refs_1_
  25.1 0.0 collective-permute-done.7.refs_3_
  25.1 5.6 %product.7 = (bf16[2,64,1024]{2,1,0:T(8,128)(2,1)S(1)}, bf16[2,64,1024]{2,1,0:T(8,128)(2,1)S(1)}, bf16[2,64,1024]{2,1,0:T(8,128)(2,1)S(1)}) custom-call(s32[4]{0:T(128)S(1)} %shift-right-arithmetic_xor_fusion.shard, bf16[2,2,32,1024]{3,2,1,0:T(8,128)(2,1)S(1)} %collective-permute-done.4.refs_0_, bf16[2,32,1024]{2,1,0:T(8,128)(2,1)S(1)} %collective-permute-done.5.refs_1_, ...), custom_call_target="tpu_custom_call" | custom-call | flops 2147483648 | bytes 8388608 | tf_op jit(solution)/shard_map/product/pallas_call | solution.py:127
  30.7 1.6 %collective-permute-start.18 = (bf16[2,64,1024]{2,1,0:T(8,128)(2,1)S(1)}, bf16[2,64,1024]{2,1,0:T(8,128)(2,1)S(1)}, u32[]{:S(2)}, u32[]{:S(2)}) collective-permute-start(bf16[2,64,1024]{2,1,0:T(8,128)(2,1)S(1)} %get-tuple-element.30), channel_id=1, source_target_pairs={{0,1},{1,0},{2,3},{3,2},{4,5},{5,4},{6,7},{7,6},{8,9},{9,8},{10,11... | collective-permute-start | bytes 786440 | tf_op jit(solution)/shard_map/ppermute | solution.py:190
  32.3 0.4 collective-permute-start.14
  32.8 1.6 %collective-permute-start.10 = (bf16[2,64,1024]{2,1,0:T(8,128)(2,1)S(1)}, bf16[2,64,1024]{2,1,0:T(8,128)(2,1)S(1)}, u32[]{:S(2)}, u32[]{:S(2)}) collective-permute-start(bf16[2,64,1024]{2,1,0:T(8,128)(2,1)S(1)} %get-tuple-element.26), channel_id=1, source_target_pairs={{0,1},{1,0},{2,3},{3,2},{4,5},{5,4},{6,7},{7,6},{8,9},{9,8},{10,11... | collective-permute-start | bytes 786440 | tf_op jit(solution)/shard_map/ppermute | solution.py:190
  34.4 2.5 %collective-permute-start.2 = (bf16[1,64,1024]{2,1,0:T(8,128)(2,1)S(1)}, bf16[1,64,1024]{2,1,0:T(8,128)(2,1)S(1)}, u32[]{:S(2)}, u32[]{:S(2)}) collective-permute-start(bf16[1,64,1024]{2,1,0:T(8,128)(2,1)S(1)} %add_convert_fusion.7), channel_id=1, source_target_pairs={{0,3},{1,2},{2,1},{3,0},{4,7},{5,6},{6,5},{7,4},{8,11},{9,10},{10,... | collective-permute-start | bytes 393224 | tf_op jit(solution)/shard_map/ppermute | solution.py:190
  36.9 5.6 %product.6 = (bf16[2,64,1024]{2,1,0:T(8,128)(2,1)S(1)}, bf16[2,64,1024]{2,1,0:T(8,128)(2,1)S(1)}, bf16[2,64,1024]{2,1,0:T(8,128)(2,1)S(1)}) custom-call(s32[4]{0:T(128)S(1)} %shift-right-arithmetic_xor_fusion.shard, bf16[2,2,32,1024]{3,2,1,0:T(8,128)(2,1)S(1)} %collective-permute-done.4.refs_0_, bf16[2,32,1024]{2,1,0:T(8,128)(2,1)S(1)} %collective-permute-done.5.refs_1_, ...), custom_call_target="tpu_custom_call" | custom-call | flops 2147483648 | bytes 8388608 | tf_op jit(solution)/shard_map/product/pallas_call | solution.py:127
  42.6 12.6 %collective-permute-done.2 = bf16[1,64,1024]{2,1,0:T(8,128)(2,1)S(1)} collective-permute-done((bf16[1,64,1024]{2,1,0:T(8,128)(2,1)S(1)}, bf16[1,64,1024]{2,1,0:T(8,128)(2,1)S(1)}, u32[]{:S(2)}, u32[]{:S(2)}) %collective-permute-start.2) | collective-permute-done | bytes 131104 | tf_op jit(solution)/shard_map/ppermute | solution.py:190
  55.2 0.1 add_convert_fusion.6
  55.2 0.1 collective-permute-start.3
  55.4 1.5 %collective-permute-start.19 = (bf16[1,64,1024]{2,1,0:T(8,128)(2,1)S(1)}, bf16[1,64,1024]{2,1,0:T(8,128)(2,1)S(1)}, u32[]{:S(2)}, u32[]{:S(2)}) collective-permute-start(bf16[1,64,1024]{2,1,0:T(8,128)(2,1)S(1)} %add_convert_fusion.1), channel_id=1, source_target_pairs={{0,3},{1,2},{2,1},{3,0},{4,7},{5,6},{6,5},{7,4},{8,11},{9,10},{10,... | collective-permute-start | bytes 393224 | tf_op jit(solution)/shard_map/ppermute | solution.py:190
  56.9 2.5 %collective-permute-start.15 = (bf16[1,64,1024]{2,1,0:T(8,128)(2,1)S(1)}, bf16[1,64,1024]{2,1,0:T(8,128)(2,1)S(1)}, u32[]{:S(2)}, u32[]{:S(2)}) collective-permute-start(bf16[1,64,1024]{2,1,0:T(8,128)(2,1)S(1)} %add_convert_fusion.3), channel_id=1, source_target_pairs={{0,3},{1,2},{2,1},{3,0},{4,7},{5,6},{6,5},{7,4},{8,11},{9,10},{10,... | collective-permute-start | bytes 393224 | tf_op jit(solution)/shard_map/ppermute | solution.py:190
  59.4 1.5 %collective-permute-start.11 = (bf16[1,64,1024]{2,1,0:T(8,128)(2,1)S(1)}, bf16[1,64,1024]{2,1,0:T(8,128)(2,1)S(1)}, u32[]{:S(2)}, u32[]{:S(2)}) collective-permute-start(bf16[1,64,1024]{2,1,0:T(8,128)(2,1)S(1)} %add_convert_fusion.5), channel_id=1, source_target_pairs={{0,3},{1,2},{2,1},{3,0},{4,7},{5,6},{6,5},{7,4},{8,11},{9,10},{10,... | collective-permute-start | bytes 393224 | tf_op jit(solution)/shard_map/ppermute | solution.py:190
  60.9 2.6 %collective-permute-done.19 = bf16[1,64,1024]{2,1,0:T(8,128)(2,1)S(1)} collective-permute-done((bf16[1,64,1024]{2,1,0:T(8,128)(2,1)S(1)}, bf16[1,64,1024]{2,1,0:T(8,128)(2,1)S(1)}, u32[]{:S(2)}, u32[]{:S(2)}) %collective-permute-start.19) | collective-permute-done | bytes 131104 | tf_op jit(solution)/shard_map/ppermute | solution.py:190
  63.5 0.1 add_convert_fusion
  63.6 1.6 %collective-permute-start.20 = (bf16[2,32,1024]{2,1,0:T(8,128)(2,1)S(1)}, bf16[2,32,1024]{2,1,0:T(8,128)(2,1)S(1)}, u32[]{:S(2)}, u32[]{:S(2)}) collective-permute-start(bf16[2,32,1024]{2,1,0:T(8,128)(2,1)S(1)} %bitcast.22), channel_id=1, source_target_pairs={{0,24},{4,28},{8,16},{12,20},{16,8},{20,12},{24,0},{28,4},{1,25},{... | collective-permute-start | bytes 393224 | tf_op jit(solution)/shard_map/ppermute | solution.py:187
  65.1 1.2 %collective-permute-done.15 = bf16[1,64,1024]{2,1,0:T(8,128)(2,1)S(1)} collective-permute-done((bf16[1,64,1024]{2,1,0:T(8,128)(2,1)S(1)}, bf16[1,64,1024]{2,1,0:T(8,128)(2,1)S(1)}, u32[]{:S(2)}, u32[]{:S(2)}) %collective-permute-start.15) | collective-permute-done | bytes 131104 | tf_op jit(solution)/shard_map/ppermute | solution.py:190
  66.3 0.1 add_convert_fusion.2
  66.4 1.6 %collective-permute-start.16 = (bf16[2,32,1024]{2,1,0:T(8,128)(2,1)S(1)}, bf16[2,32,1024]{2,1,0:T(8,128)(2,1)S(1)}, u32[]{:S(2)}, u32[]{:S(2)}) collective-permute-start(bf16[2,32,1024]{2,1,0:T(8,128)(2,1)S(1)} %bitcast.23), channel_id=1, source_target_pairs={{0,16},{4,20},{8,24},{12,28},{16,0},{20,4},{24,8},{28,12},{1,17},{... | collective-permute-start | bytes 393224 | tf_op jit(solution)/shard_map/ppermute | solution.py:187
  68.0 0.8 %collective-permute-done.11 = bf16[1,64,1024]{2,1,0:T(8,128)(2,1)S(1)} collective-permute-done((bf16[1,64,1024]{2,1,0:T(8,128)(2,1)S(1)}, bf16[1,64,1024]{2,1,0:T(8,128)(2,1)S(1)}, u32[]{:S(2)}, u32[]{:S(2)}) %collective-permute-start.11) | collective-permute-done | bytes 131104 | tf_op jit(solution)/shard_map/ppermute | solution.py:190
  68.7 0.1 add_convert_fusion.4
  68.8 1.2 %collective-permute-start.12 = (bf16[2,32,1024]{2,1,0:T(8,128)(2,1)S(1)}, bf16[2,32,1024]{2,1,0:T(8,128)(2,1)S(1)}, u32[]{:S(2)}, u32[]{:S(2)}) collective-permute-start(bf16[2,32,1024]{2,1,0:T(8,128)(2,1)S(1)} %bitcast.24), channel_id=1, source_target_pairs={{0,8},{4,12},{8,0},{12,4},{16,24},{20,28},{24,16},{28,20},{1,9},{5... | collective-permute-start | bytes 393224 | tf_op jit(solution)/shard_map/ppermute | solution.py:187
  70.0 0.1 collective-permute-start.21
  70.1 2.2 %collective-permute-done.16.refs_4_ = bf16[2,32,1024]{2,1,0:T(8,128)(2,1)S(1)} collective-permute-done((bf16[2,32,1024]{2,1,0:T(8,128)(2,1)S(1)}, bf16[2,32,1024]{2,1,0:T(8,128)(2,1)S(1)}, u32[]{:S(2)}, u32[]{:S(2)}) %collective-permute-start.16) | collective-permute-done | bytes 131104 | tf_op jit(solution)/shard_map/ppermute | solution.py:187
  72.3 0.0 collective-permute-start.17
  72.3 1.6 %collective-permute-done.12.refs_2_ = bf16[2,32,1024]{2,1,0:T(8,128)(2,1)S(1)} collective-permute-done((bf16[2,32,1024]{2,1,0:T(8,128)(2,1)S(1)}, bf16[2,32,1024]{2,1,0:T(8,128)(2,1)S(1)}, u32[]{:S(2)}, u32[]{:S(2)}) %collective-permute-start.12) | collective-permute-done | bytes 131104 | tf_op jit(solution)/shard_map/ppermute | solution.py:187
  74.0 0.0 collective-permute-start.13
  74.0 0.0 collective-permute-done.3.refs_1_
  74.0 1.2 %collective-permute-done.13.refs_3_ = bf16[32,1024]{1,0:T(8,128)(2,1)S(1)} collective-permute-done((bf16[32,1024]{1,0:T(8,128)(2,1)S(1)}, bf16[32,1024]{1,0:T(8,128)(2,1)S(1)}, u32[]{:S(2)}, u32[]{:S(2)}) %collective-permute-start.13) | collective-permute-done | bytes 65568 | tf_op jit(solution)/shard_map/ppermute | solution.py:187
  75.2 1.1 %order.1 = bf16[256,1024]{1,0:T(8,128)(2,1)} custom-call(bf16[256,256]{1,0:T(8,128)(2,1)S(1)} %fusion.place, bf16[2,32,1024]{2,1,0:T(8,128)(2,1)S(1)} %bitcast.21, bf16[32,1024]{1,0:T(8,128)(2,1)S(1)} %collective-permute-done.3.refs_1_, bf16[2,32,1024]{2,1,0:T(8,128)(2,1)S(1)} %collective-permute-done.12.refs_2_, ...), custom_call_target="tpu_custom_call" | custom-call | tf_op jit(solution)/shard_map/order/pallas_call | solution.py:162
  (24 shorter events, 0.2 us)
Async XLA Ops:
  2.5 14.4 %collective-permute-start.4 = (bf16[2,2,32,1024]{3,2,1,0:T(8,128)(2,1)}, bf16[2,2,32,1024]{3,2,1,0:T(8,128)(2,1)S(1)}, u32[]{:S(2)}, u32[]{:S(2)}) collective-permute-start(bf16[2,2,32,1024]{3,2,1,0:T(8,128)(2,1)} %get-tuple-element.22), channel_id=1, source_target_pairs={{0,8},{4,12},{8,0},{12,4},{16,24},{20,28},{24,16},{28,20},{1,9},{5... | collective-permute-start | bytes 786440 | tf_op jit(solution)/shard_map/ppermute | solution.py:187
  5.5 13.6 %collective-permute-start.6 = (bf16[2,2,32,1024]{3,2,1,0:T(8,128)(2,1)}, bf16[2,2,32,1024]{3,2,1,0:T(8,128)(2,1)S(1)}, u32[]{:S(2)}, u32[]{:S(2)}) collective-permute-start(bf16[2,2,32,1024]{3,2,1,0:T(8,128)(2,1)} %get-tuple-element.23), channel_id=1, source_target_pairs={{0,16},{4,20},{8,24},{12,28},{16,0},{20,4},{24,8},{28,12},{1,17},{... | collective-permute-start | bytes 786440 | tf_op jit(solution)/shard_map/ppermute | solution.py:187
  7.0 12.2 %collective-permute-start.8 = (bf16[2,2,32,1024]{3,2,1,0:T(8,128)(2,1)}, bf16[2,2,32,1024]{3,2,1,0:T(8,128)(2,1)S(1)}, u32[]{:S(2)}, u32[]{:S(2)}) collective-permute-start(bf16[2,2,32,1024]{3,2,1,0:T(8,128)(2,1)} %get-tuple-element.24), channel_id=1, source_target_pairs={{0,24},{4,28},{8,16},{12,20},{16,8},{20,12},{24,0},{28,4},{1,25},{... | collective-permute-start | bytes 786440 | tf_op jit(solution)/shard_map/ppermute | solution.py:187
  7.1 1.6 %collective-permute-start = (bf16[2,32,1024]{2,1,0:T(8,128)(2,1)}, bf16[2,32,1024]{2,1,0:T(8,128)(2,1)S(1)}, u32[]{:S(2)}, u32[]{:S(2)}) collective-permute-start(bf16[2,32,1024]{2,1,0:T(8,128)(2,1)} %get-tuple-element.19), channel_id=1, source_target_pairs={{0,4},{4,0},{8,12},{12,8},{16,20},{20,16},{24,28},{28,24},{1,5},{5... | collective-permute-start | bytes 393224 | tf_op jit(solution)/shard_map/ppermute | solution.py:187
  8.6 0.9 %copy-start = (bf16[2,32,1024]{2,1,0:T(8,128)(2,1)S(1)}, bf16[2,32,1024]{2,1,0:T(8,128)(2,1)}, u32[]{:S(2)}) copy-start(bf16[2,32,1024]{2,1,0:T(8,128)(2,1)} %get-tuple-element.18.refs_0_) | copy-start | bytes 393220
  14.8 19.6 %collective-permute-start.1 = (bf16[2,64,1024]{2,1,0:T(8,128)(2,1)S(1)}, bf16[2,64,1024]{2,1,0:T(8,128)(2,1)S(1)}, u32[]{:S(2)}, u32[]{:S(2)}) collective-permute-start(bf16[2,64,1024]{2,1,0:T(8,128)(2,1)S(1)} %product.5), channel_id=1, source_target_pairs={{0,1},{1,0},{2,3},{3,2},{4,5},{5,4},{6,7},{7,6},{8,9},{9,8},{10,11... | collective-permute-start | bytes 786440 | tf_op jit(solution)/shard_map/ppermute | solution.py:190
  16.9 8.1 %collective-permute-start.5 = (bf16[2,32,1024]{2,1,0:T(8,128)(2,1)S(1)}, bf16[2,32,1024]{2,1,0:T(8,128)(2,1)S(1)}, u32[]{:S(2)}, u32[]{:S(2)}) collective-permute-start(bf16[2,32,1024]{2,1,0:T(8,128)(2,1)S(1)} %slice_bitcast_fusion.2), channel_id=1, source_target_pairs={{0,4},{4,0},{8,12},{12,8},{16,20},{20,16},{24,28},{28,24},{1,5},{5... | collective-permute-start | bytes 393224 | tf_op jit(solution)/shard_map/ppermute | solution.py:187
  19.1 5.9 %collective-permute-start.7 = (bf16[2,32,1024]{2,1,0:T(8,128)(2,1)S(1)}, bf16[2,32,1024]{2,1,0:T(8,128)(2,1)S(1)}, u32[]{:S(2)}, u32[]{:S(2)}) collective-permute-start(bf16[2,32,1024]{2,1,0:T(8,128)(2,1)S(1)} %slice_bitcast_fusion.1), channel_id=1, source_target_pairs={{0,4},{4,0},{8,12},{12,8},{16,20},{20,16},{24,28},{28,24},{1,5},{5... | collective-permute-start | bytes 393224 | tf_op jit(solution)/shard_map/ppermute | solution.py:187
  19.2 5.8 %collective-permute-start.9 = (bf16[2,32,1024]{2,1,0:T(8,128)(2,1)S(1)}, bf16[2,32,1024]{2,1,0:T(8,128)(2,1)S(1)}, u32[]{:S(2)}, u32[]{:S(2)}) collective-permute-start(bf16[2,32,1024]{2,1,0:T(8,128)(2,1)S(1)} %slice_bitcast_fusion), channel_id=1, source_target_pairs={{0,4},{4,0},{8,12},{12,8},{16,20},{20,16},{24,28},{28,24},{1,5},{5... | collective-permute-start | bytes 393224 | tf_op jit(solution)/shard_map/ppermute | solution.py:187
  30.7 24.6 %collective-permute-start.18 = (bf16[2,64,1024]{2,1,0:T(8,128)(2,1)S(1)}, bf16[2,64,1024]{2,1,0:T(8,128)(2,1)S(1)}, u32[]{:S(2)}, u32[]{:S(2)}) collective-permute-start(bf16[2,64,1024]{2,1,0:T(8,128)(2,1)S(1)} %get-tuple-element.30), channel_id=1, source_target_pairs={{0,1},{1,0},{2,3},{3,2},{4,5},{5,4},{6,7},{7,6},{8,9},{9,8},{10,11... | collective-permute-start | bytes 786440 | tf_op jit(solution)/shard_map/ppermute | solution.py:190
  32.3 24.5 %collective-permute-start.14 = (bf16[2,64,1024]{2,1,0:T(8,128)(2,1)S(1)}, bf16[2,64,1024]{2,1,0:T(8,128)(2,1)S(1)}, u32[]{:S(2)}, u32[]{:S(2)}) collective-permute-start(bf16[2,64,1024]{2,1,0:T(8,128)(2,1)S(1)} %get-tuple-element.28), channel_id=1, source_target_pairs={{0,1},{1,0},{2,3},{3,2},{4,5},{5,4},{6,7},{7,6},{8,9},{9,8},{10,11... | collective-permute-start | bytes 786440 | tf_op jit(solution)/shard_map/ppermute | solution.py:190
  32.8 26.6 %collective-permute-start.10 = (bf16[2,64,1024]{2,1,0:T(8,128)(2,1)S(1)}, bf16[2,64,1024]{2,1,0:T(8,128)(2,1)S(1)}, u32[]{:S(2)}, u32[]{:S(2)}) collective-permute-start(bf16[2,64,1024]{2,1,0:T(8,128)(2,1)S(1)} %get-tuple-element.26), channel_id=1, source_target_pairs={{0,1},{1,0},{2,3},{3,2},{4,5},{5,4},{6,7},{7,6},{8,9},{9,8},{10,11... | collective-permute-start | bytes 786440 | tf_op jit(solution)/shard_map/ppermute | solution.py:190
  34.4 20.8 %collective-permute-start.2 = (bf16[1,64,1024]{2,1,0:T(8,128)(2,1)S(1)}, bf16[1,64,1024]{2,1,0:T(8,128)(2,1)S(1)}, u32[]{:S(2)}, u32[]{:S(2)}) collective-permute-start(bf16[1,64,1024]{2,1,0:T(8,128)(2,1)S(1)} %add_convert_fusion.7), channel_id=1, source_target_pairs={{0,3},{1,2},{2,1},{3,0},{4,7},{5,6},{6,5},{7,4},{8,11},{9,10},{10,... | collective-permute-start | bytes 393224 | tf_op jit(solution)/shard_map/ppermute | solution.py:190
  55.2 18.7 %collective-permute-start.3 = (bf16[32,1024]{1,0:T(8,128)(2,1)S(1)}, bf16[32,1024]{1,0:T(8,128)(2,1)S(1)}, u32[]{:S(2)}, u32[]{:S(2)}) collective-permute-start(bf16[32,1024]{1,0:T(8,128)(2,1)S(1)} %slice_bitcast_fusion.6), channel_id=1, source_target_pairs={{0,4},{4,0},{8,12},{12,8},{16,20},{20,16},{24,28},{28,24},{1,5},{5... | collective-permute-start | bytes 196616 | tf_op jit(solution)/shard_map/ppermute | solution.py:187
  55.4 8.2 %collective-permute-start.19 = (bf16[1,64,1024]{2,1,0:T(8,128)(2,1)S(1)}, bf16[1,64,1024]{2,1,0:T(8,128)(2,1)S(1)}, u32[]{:S(2)}, u32[]{:S(2)}) collective-permute-start(bf16[1,64,1024]{2,1,0:T(8,128)(2,1)S(1)} %add_convert_fusion.1), channel_id=1, source_target_pairs={{0,3},{1,2},{2,1},{3,0},{4,7},{5,6},{6,5},{7,4},{8,11},{9,10},{10,... | collective-permute-start | bytes 393224 | tf_op jit(solution)/shard_map/ppermute | solution.py:190
  56.9 9.5 %collective-permute-start.15 = (bf16[1,64,1024]{2,1,0:T(8,128)(2,1)S(1)}, bf16[1,64,1024]{2,1,0:T(8,128)(2,1)S(1)}, u32[]{:S(2)}, u32[]{:S(2)}) collective-permute-start(bf16[1,64,1024]{2,1,0:T(8,128)(2,1)S(1)} %add_convert_fusion.3), channel_id=1, source_target_pairs={{0,3},{1,2},{2,1},{3,0},{4,7},{5,6},{6,5},{7,4},{8,11},{9,10},{10,... | collective-permute-start | bytes 393224 | tf_op jit(solution)/shard_map/ppermute | solution.py:190
  59.4 9.3 %collective-permute-start.11 = (bf16[1,64,1024]{2,1,0:T(8,128)(2,1)S(1)}, bf16[1,64,1024]{2,1,0:T(8,128)(2,1)S(1)}, u32[]{:S(2)}, u32[]{:S(2)}) collective-permute-start(bf16[1,64,1024]{2,1,0:T(8,128)(2,1)S(1)} %add_convert_fusion.5), channel_id=1, source_target_pairs={{0,3},{1,2},{2,1},{3,0},{4,7},{5,6},{6,5},{7,4},{8,11},{9,10},{10,... | collective-permute-start | bytes 393224 | tf_op jit(solution)/shard_map/ppermute | solution.py:190
  63.6 6.4 %collective-permute-start.20 = (bf16[2,32,1024]{2,1,0:T(8,128)(2,1)S(1)}, bf16[2,32,1024]{2,1,0:T(8,128)(2,1)S(1)}, u32[]{:S(2)}, u32[]{:S(2)}) collective-permute-start(bf16[2,32,1024]{2,1,0:T(8,128)(2,1)S(1)} %bitcast.22), channel_id=1, source_target_pairs={{0,24},{4,28},{8,16},{12,20},{16,8},{20,12},{24,0},{28,4},{1,25},{... | collective-permute-start | bytes 393224 | tf_op jit(solution)/shard_map/ppermute | solution.py:187
  66.4 5.9 %collective-permute-start.16 = (bf16[2,32,1024]{2,1,0:T(8,128)(2,1)S(1)}, bf16[2,32,1024]{2,1,0:T(8,128)(2,1)S(1)}, u32[]{:S(2)}, u32[]{:S(2)}) collective-permute-start(bf16[2,32,1024]{2,1,0:T(8,128)(2,1)S(1)} %bitcast.23), channel_id=1, source_target_pairs={{0,16},{4,20},{8,24},{12,28},{16,0},{20,4},{24,8},{28,12},{1,17},{... | collective-permute-start | bytes 393224 | tf_op jit(solution)/shard_map/ppermute | solution.py:187
  68.8 5.2 %collective-permute-start.12 = (bf16[2,32,1024]{2,1,0:T(8,128)(2,1)S(1)}, bf16[2,32,1024]{2,1,0:T(8,128)(2,1)S(1)}, u32[]{:S(2)}, u32[]{:S(2)}) collective-permute-start(bf16[2,32,1024]{2,1,0:T(8,128)(2,1)S(1)} %bitcast.24), channel_id=1, source_target_pairs={{0,8},{4,12},{8,0},{12,4},{16,24},{20,28},{24,16},{28,20},{1,9},{5... | collective-permute-start | bytes 393224 | tf_op jit(solution)/shard_map/ppermute | solution.py:187
  70.0 4.0 %collective-permute-start.21 = (bf16[32,1024]{1,0:T(8,128)(2,1)S(1)}, bf16[32,1024]{1,0:T(8,128)(2,1)S(1)}, u32[]{:S(2)}, u32[]{:S(2)}) collective-permute-start(bf16[32,1024]{1,0:T(8,128)(2,1)S(1)} %slice_bitcast_fusion.3), channel_id=1, source_target_pairs={{0,4},{4,0},{8,12},{12,8},{16,20},{20,16},{24,28},{28,24},{1,5},{5... | collective-permute-start | bytes 196616 | tf_op jit(solution)/shard_map/ppermute | solution.py:187
  72.3 1.7 %collective-permute-start.17 = (bf16[32,1024]{1,0:T(8,128)(2,1)S(1)}, bf16[32,1024]{1,0:T(8,128)(2,1)S(1)}, u32[]{:S(2)}, u32[]{:S(2)}) collective-permute-start(bf16[32,1024]{1,0:T(8,128)(2,1)S(1)} %slice_bitcast_fusion.4), channel_id=1, source_target_pairs={{0,4},{4,0},{8,12},{12,8},{16,20},{20,16},{24,28},{28,24},{1,5},{5... | collective-permute-start | bytes 196616 | tf_op jit(solution)/shard_map/ppermute | solution.py:187
  74.0 1.3 %collective-permute-start.13 = (bf16[32,1024]{1,0:T(8,128)(2,1)S(1)}, bf16[32,1024]{1,0:T(8,128)(2,1)S(1)}, u32[]{:S(2)}, u32[]{:S(2)}) collective-permute-start(bf16[32,1024]{1,0:T(8,128)(2,1)S(1)} %slice_bitcast_fusion.5), channel_id=1, source_target_pairs={{0,4},{4,0},{8,12},{12,8},{16,20},{20,16},{24,28},{28,24},{1,5},{5... | collective-permute-start | bytes 196616 | tf_op jit(solution)/shard_map/ppermute | solution.py:187

commit v2 on v1

v2 whole, which is shorter than its diff:
```python
import functools

import jax
import jax.numpy as jnp
from jax import lax
from jax.experimental import pallas as pl
from jax.experimental.pallas import tpu as pltpu
from jax.sharding import PartitionSpec as P

PART = 512
PIECE = 256
LIMIT = 48 << 20
WHOLE = 60 << 20


def pick_kernel(peers, *refs):
    given, outs = refs[:4], refs[4 : 4 + peers]
    amp_tiles, cd_tiles, q_owner, amps, held, slots, sems = refs[4 + peers :]
    copies = [
        pltpu.make_async_copy(source, target, sems.at[i])
        for i, (source, target) in enumerate(zip(given, (amp_tiles, cd_tiles, q_owner, amps)))
    ]
    for copy in copies:
        copy.start()
    for copy in copies[:3]:
        copy.wait()
    width = amps.shape[1]
    wants = cd_tiles.shape[0]
    me = lax.axis_index("wide")

    def look(q, carry):
        peer = q_owner[q] ^ me
        for k in range(wants):
            slot = jnp.int32(width)
            for t in range(width):
                slot = jnp.where(amp_tiles[t, me] == cd_tiles[k, q], t, slot)
            slots[peer, k] = slot
        return carry

    lax.fori_loop(0, peers, look, 0)
    copies[3].wait()
    for t in range(width):
        held[t] = amps[:, t, :]
    held[width] = jnp.zeros_like(held[width])
    for j in range(peers):
        for k in range(wants):
            outs[j][k] = held[slots[j, k]]


def pick(amplitudes, amp_tiles, cd_tiles, q_owner):
    rows, width, depth = amplitudes.shape
    peers, wants = cd_tiles.shape
    return pl.pallas_call(
        functools.partial(pick_kernel, peers),
        out_shape=[jax.ShapeDtypeStruct((wants, rows, depth), jnp.bfloat16)] * peers,
        in_specs=[pl.BlockSpec(memory_space=pltpu.HBM)] * 4,
        out_specs=[pl.BlockSpec(memory_space=pltpu.VMEM)] * peers,
        scratch_shapes=[
            pltpu.SMEM((width, amp_tiles.shape[0]), jnp.int32),
            pltpu.SMEM((wants, peers), jnp.int32),
            pltpu.SMEM((peers,), jnp.int32),
            pltpu.VMEM(amplitudes.shape, jnp.bfloat16),
            pltpu.VMEM((width + 1, rows, depth), jnp.bfloat16),
            pltpu.SMEM((peers, wants), jnp.int32),
            pltpu.SemaphoreType.DMA((4,)),
        ],
        compiler_params=pltpu.CompilerParams(vmem_limit_bytes=WHOLE),
        name="pick",
    )(amp_tiles.T, cd_tiles.T, q_owner, amplitudes)


def product_kernel(count, chunks, others, order, shard, *refs):
    picked, ints, outs = refs[:count], refs[count], refs[count + 1 + others : count + 1 + others + chunks]
    buffer, left, sems, row_sems = refs[-4:]
    shares, wants, share, depth = buffer.shape
    rows = picked[0].shape[1]
    pieces = sems.shape[2]
    piece = share // pieces

    def copy(s, k, p):
        start = pl.multiple_of(shard[order[s]] * share, share) + p * piece
        return pltpu.make_async_copy(
            ints.at[0, k, pl.ds(start, piece), :], buffer.at[s, k, pl.ds(p * piece, piece), :], sems.at[s, k, p]
        )

    placing = [
        pltpu.make_async_copy(ref.at[k], left.at[k, i * rows : (i + 1) * rows, :], row_sems.at[k, i])
        for k in range(wants)
        for i, ref in enumerate(picked)
    ]
    for row_copy in placing:
        row_copy.start()
    for s in range(shares):
        for p in range(pieces):
            for k in range(wants):
                copy(s, k, p).start()
    for row_copy in placing:
        row_copy.wait()

    each = count * rows // chunks
    part = min(PART, share)
    for s in range(shares):
        for i in range(share // part):
            at = slice(i * part, (i + 1) * part)
            for p in range(i * part // piece, (i + 1) * part // piece):
                for k in range(wants):
                    copy(s, k, p).wait()
            total = None
            for k in range(wants):
                term = lax.dot_general(
                    left[k], buffer[s, k, at, :], (((1,), (1,)), ((), ())), preferred_element_type=jnp.float32
                )
                total = term if total is None else total + term
            total = total.astype(jnp.bfloat16)
            for c in range(chunks):
                outs[c][s, :, at] = total[c * each : (c + 1) * each]


def product(shard, order, picked, ints, chunks, passed, after, limit):
    _, wants, pairs, depth = ints.shape
    rows = picked[0].shape[1]
    share = pairs // shard.shape[0]
    count = len(picked)
    shares = len(order)
    pieces = max(1, share // PIECE)
    vmem, any_space = pl.BlockSpec(memory_space=pltpu.VMEM), pl.BlockSpec(memory_space=pl.ANY)
    outs = pl.pallas_call(
        functools.partial(product_kernel, count, chunks, len(passed) + len(after), order),
        out_shape=[jax.ShapeDtypeStruct((shares, count * rows // chunks, share), jnp.bfloat16)] * chunks
        + [jax.ShapeDtypeStruct(p.shape, p.dtype) for p in passed],
        in_specs=[pl.BlockSpec(memory_space=pltpu.SMEM)] + [any_space] * (count + 1 + len(passed) + len(after)),
        out_specs=[vmem] * chunks + [any_space] * len(passed),
        input_output_aliases={2 + count + i: chunks + i for i in range(len(passed))},
        scratch_shapes=[
            pltpu.VMEM((shares, wants, share, depth), jnp.bfloat16),
            pltpu.VMEM((wants, count * rows, depth), jnp.bfloat16),
            pltpu.SemaphoreType.DMA((shares, wants, pieces)),
            pltpu.SemaphoreType.DMA((wants, count)),
        ],
        compiler_params=pltpu.CompilerParams(vmem_limit_bytes=limit),
        cost_estimate=pl.CostEstimate(
            flops=2 * 256 * wants * depth * share * shares,
            bytes_accessed=2 * wants * depth * share * shares,
            transcendentals=0,
        ),
        name="product",
    )(shard, *picked, ints, *passed, *after)
    return outs[:chunks], outs[chunks:]


def add(*terms):
    return sum(t.astype(jnp.float32) for t in terms).astype(jnp.bfloat16)


def order_kernel(place, *refs):
    shares, out, held = refs[:-2], refs[-2], refs[-1]
    rows = shares[0].shape[0]
    for j, share in enumerate(shares):
        held[j * rows : (j + 1) * rows, :] = share[...]
    out[...] = jnp.dot(place[...], held[...], preferred_element_type=jnp.float32).astype(jnp.bfloat16)


def order(place, shares):
    size, share = place.shape[0], shares[0].shape[-1]
    vmem = pl.BlockSpec(memory_space=pltpu.VMEM)
    return pl.pallas_call(
        order_kernel,
        out_shape=jax.ShapeDtypeStruct((size, share), jnp.bfloat16),
        in_specs=[vmem] * (1 + len(shares)),
        out_specs=vmem,
        scratch_shapes=[pltpu.VMEM((size, share), jnp.bfloat16)],
        compiler_params=pltpu.CompilerParams(vmem_limit_bytes=LIMIT),
        name="order",
    )(place, *shares)


def on_device(amplitudes, amp_tiles, integrals, cd_tiles, q_owner):
    peers = lax.axis_size("wide")
    devices = lax.axis_size("narrow")
    rows = amplitudes.shape[0]
    at = lax.axis_index("narrow")

    gray = at ^ (at >> 1)
    code = jnp.arange(devices, dtype=jnp.int32) ^ gray
    shard, shift = code, code >> 1
    for _ in range(devices.bit_length() - 2):
        shard, shift = shard ^ shift, shift >> 1
    odd, middle, home = tuple(range(1, devices, 2)), tuple(range(2, devices, 2)), (0,)

    def swap(value, j):
        return lax.ppermute(value, "wide", [(w, w ^ j) for w in range(peers)])

    def swap_line(value, mask):
        return lax.ppermute(value, "narrow", [(n, n ^ mask) for n in range(devices)])

    def first_step(message):
        return dict(zip(odd, swap_line(message, 1)))

    def later_steps(kept, got):
        terms = {0: [got[1]]}
        for r, value in zip(middle, kept):
            terms[r] = [value, got[r ^ 1]]
        messages = []
        step = 1
        while 1 << step < devices:
            names = [r for r in sorted(terms) if r >> step & 1]
            messages.append(jnp.stack([add(*terms.pop(r)) for r in names]))
            for r, value in zip(names, swap_line(messages[-1], (2 << step) - 1)):
                terms[r ^ (1 << step)].append(value)
            step += 1
        return messages[0], terms[0]

    chips = peers // 2
    near = [g for g in range(1, chips) if g & (g - 1) == 0]
    far = [g for g in range(1, chips) if g & (g - 1)]

    def of(groups):
        return [j for g in groups for j in (2 * g, 2 * g + 1)]

    def multiply(names, groups, passed=(), after=(), limit=LIMIT):
        chosen = [lot[j] for j in of(groups)]
        outs, passed = product(shard, names, chosen, integrals, len(groups), list(passed), list(after), limit)
        return dict(zip(groups, outs)), passed

    lot = dict(enumerate(pick(amplitudes, amp_tiles, cd_tiles, q_owner)))
    for j in [1] + of(near):
        lot[j] = swap(lot[j], j)
    wide = jnp.arange(peers * rows, dtype=jnp.int32)
    source = (q_owner ^ lax.axis_index("wide"))[None, :] * rows + jnp.arange(rows, dtype=jnp.int32)[:, None]
    place = (source.reshape(-1, 1) == wide[None, :]).astype(jnp.bfloat16)

    got, ready, sums = {}, {}, {}
    away, _ = multiply(odd, [0])
    got[0] = first_step(away[0])
    outs, passed = multiply(odd, near, [lot[j] for j in of(far)], [away[0]])
    lot.update((j, swap(value, j)) for j, value in zip(of(far), passed))
    away.update(outs)
    first, others = near[0], near[1:]
    got[first] = first_step(away[first])
    kept, passed = multiply(middle, [0] + near, [away[g] for g in others])
    got.update((g, first_step(value)) for g, value in zip(others, passed))
    ready[0], sums[0] = later_steps(kept[0], got[0])
    outs, _ = multiply(odd, far, after=[ready[0]])
    away.update(outs)
    got.update((g, first_step(value)) for g, value in outs.items())
    ready[first], sums[first] = later_steps(kept[first], got[first])
    outs, _ = multiply(middle, far, after=[away[far[0]], ready[first]])
    kept.update(outs)
    for g in others + far:
        ready[g], sums[g] = later_steps(kept[g], got[g])
    own, _ = multiply(home, range(chips), after=[ready[g] for g in others] + [kept[far[0]], place])

    shares = {}
    for g in [0] + near + far:
        total = add(own[g][0], *sums[g]).reshape(2, rows, -1)
        for c in range(2):
            j = 2 * g + c
            shares[j] = swap(total[c], j) if j else total[c]
    return order(place, [shares[j] for j in range(peers)]).reshape(rows, peers, -1)


def solution(mesh):
    placed = (P("wide", None, "narrow"), P(), P("wide", None, None, "narrow"), P(), P())
    return jax.shard_map(
        on_device, mesh=mesh, in_specs=placed, out_specs=P("wide", None, "narrow"), check_vma=False
    )
```

time: 76.5 us -> 75.9 us (level)
  waiting for transfers between devices: 25.1 us -> 9.58 us
  Pallas kernels: 25.3 us -> 35.4 us
  starting transfers between devices: 23.4 us -> 27.9 us
    ppermute x8, waiting for transfers between devices: 17.2 us -> 5.77 us  [swap_line(): lax.ppermute(value, 'narrow', [(n, n ^ mask) for n in range(devices)])]
    pallas_call x5 -> x7, Pallas kernels: 22.8 us -> 32.9 us  [the longest x6 31.8 us: product(): pl.pallas_call(functools.partial(product_kernel, count, chunks, len(passe...]
    ppermute x14, starting transfers between devices: 9.71 us -> 13.9 us  [swap(): return lax.ppermute(value, 'wide', [(w, w ^ j) for w in range(peers)])]
    ppermute x14, waiting for transfers between devices: 7.91 us -> 3.81 us  [swap(): return lax.ppermute(value, 'wide', [(w, w ^ j) for w in range(peers)])]
  transfers between devices with their start and end apart: 22 -> 22, of which waited for: 9 -> 4; matrix products, arithmetic and copies ran while one was open for 2% -> 2% of each run, Pallas kernels for 28% -> 42%
where the time goes in v2:
time: 75.9 us; the launch traced here: 75.4 us
  Pallas kernels  35.4 us (47%)
  starting transfers between devices  27.9 us (37%)
  waiting for transfers between devices  9.58 us (13%)
  other arithmetic  1.15 us (2%)
  local copies, waits for them, and re-layouts  1.04 us (1%)
    pallas_call x6, Pallas kernels, product(): pl.pallas_call(functools.partial(product_kernel, count, chunks, len(passe...  31.8 us
    ppermute x8, starting transfers between devices, swap_line(): lax.ppermute(value, 'narrow', [(n, n ^ mask) for n in range(devices)])  14 us
    ppermute x14, starting transfers between devices, swap(): return lax.ppermute(value, 'wide', [(w, w ^ j) for w in range(peers)])  13.9 us
    ppermute x8, waiting for transfers between devices, swap_line(): lax.ppermute(value, 'narrow', [(n, n ^ mask) for n in range(devices)])  5.77 us
    ppermute x14, waiting for transfers between devices, swap(): return lax.ppermute(value, 'wide', [(w, w ^ j) for w in range(peers)])  3.81 us
    pallas_call x1, Pallas kernels, pick(): pl.pallas_call(functools.partial(pick_kernel, peers), out_shape=[jax.Shap...  2.51 us
  transfers between devices with their start and end apart: 22, of which 4 were waited for; matrix products, arithmetic and copies ran while one was open for 2% of the time, Pallas kernels for 42%

profile of v2, /device:TPU:0, one launch (start us, length us, event | category | flops | bytes accessed | tf_op | source)
XLA Modules:
  0.0 75.4 jit_solution(11759619535747652846)
XLA Ops:
  0.0 2.5 %pick.1 = (bf16[2,32,1024]{2,1,0:T(8,128)(2,1)}, bf16[2,32,1024]{2,1,0:T(8,128)(2,1)}, bf16[2,32,1024]{2,1,0:T(8,128)(2,1)}, bf16[2,32,1024]{2,1,0:T(8,128)(2,1)...) custom-call(s32[4,8]{1,0:T(4,128)} %bitcast.19, ...), custom_call_target="tpu_custom_call" | custom-call | tf_op jit(solution)/shard_map/pick/pallas_call | solution.py:53
  2.5 0.5 collective-permute-start
  3.0 2.6 %collective-permute-start.1 = (bf16[2,32,1024]{2,1,0:T(8,128)(2,1)}, bf16[2,32,1024]{2,1,0:T(8,128)(2,1)S(1)}, u32[]{:S(2)}, u32[]{:S(2)}) collective-permute-start(bf16[2,32,1024]{2,1,0:T(8,128)(2,1)} %get-tuple-element.27), channel_id=1, source_target_pairs={{0,8},{4,12},{8,0},{12,4},{16,24},{20,28},{24,16},{28,20},{1,9},{5... | collective-permute-start | bytes 393224 | tf_op jit(solution)/shard_map/ppermute | solution.py:191
  5.6 0.1 collective-permute-start.2
  5.7 1.8 %collective-permute-start.3 = (bf16[2,32,1024]{2,1,0:T(8,128)(2,1)}, bf16[2,32,1024]{2,1,0:T(8,128)(2,1)S(1)}, u32[]{:S(2)}, u32[]{:S(2)}) collective-permute-start(bf16[2,32,1024]{2,1,0:T(8,128)(2,1)} %get-tuple-element.29), channel_id=1, source_target_pairs={{0,16},{4,20},{8,24},{12,28},{16,0},{20,4},{24,8},{28,12},{1,17},{... | collective-permute-start | bytes 393224 | tf_op jit(solution)/shard_map/ppermute | solution.py:191
  7.4 0.0 collective-permute-start.4
  7.5 0.7 xor_multiply_fusion
  8.1 0.1 add.71
  8.2 0.1 fusion.refs_11_.place
  8.4 0.0 copy-start
  8.4 0.9 %copy-done = bf16[2,32,1024]{2,1,0:T(8,128)(2,1)S(1)} copy-done((bf16[2,32,1024]{2,1,0:T(8,128)(2,1)S(1)}, bf16[2,32,1024]{2,1,0:T(8,128)(2,1)}, u32[]{:S(2)}) %copy-start) | copy-done | bytes 131096
  9.3 5.6 %product.6.refs_7_ = bf16[2,64,1024]{2,1,0:T(8,128)(2,1)S(1)} custom-call(s32[4]{0:T(128)S(1)} %shift-right-arithmetic_xor_fusion.shard, bf16[2,32,1024]{2,1,0:T(8,128)(2,1)S(1)} %copy-done, bf16[2,32,1024]{2,1,0:T(8,128)(2,1)S(1)} %collective-permute-done.refs_1_, bf16[1,2,4096,1024]{3,2,1,0:T(8,128)(2,1)} %refs_8_.1), custom_call_target="tpu_custom_call" | custom-call | flops 2147483648 | bytes 8388608 | tf_op jit(solution)/shard_map/product/pallas_call | solution.py:127
  14.9 1.8 %collective-permute-start.8 = (bf16[2,64,1024]{2,1,0:T(8,128)(2,1)S(1)}, bf16[2,64,1024]{2,1,0:T(8,128)(2,1)S(1)}, u32[]{:S(2)}, u32[]{:S(2)}) collective-permute-start(bf16[2,64,1024]{2,1,0:T(8,128)(2,1)S(1)} %product.6.refs_7_), channel_id=1, source_target_pairs={{0,1},{1,0},{2,3},{3,2},{4,5},{5,4},{6,7},{7,6},{8,9},{9,8},{10,11... | collective-permute-start | bytes 786440 | tf_op jit(solution)/shard_map/ppermute | solution.py:194
  16.7 0.0 collective-permute-done.3.refs_2_.refs_4_
  16.7 6.3 %product.7 = (bf16[2,64,1024]{2,1,0:T(8,128)(2,1)S(1)}, bf16[2,64,1024]{2,1,0:T(8,128)(2,1)S(1)}, bf16[2,32,1024]{2,1,0:T(8,128)(2,1)S(1)}, bf16[2,32,1024]{2,1,0:T(8,128)(2,1)S(1)}) custom-call(s32[4]{0:T(128)S(1)} %shift-right-arithmetic_xor_fusion.shard, ...), custom_call_target="tpu_custom_call", output_to_operand_aliasing={{2}: (6, {}), {3}: (7, {})} | custom-call | flops 2147483648 | bytes 8388608 | tf_op jit(solution)/shard_map/product/pallas_call | solution.py:127
  23.0 2.5 %collective-permute-start.5 = (bf16[2,32,1024]{2,1,0:T(8,128)(2,1)S(1)}, bf16[2,32,1024]{2,1,0:T(8,128)(2,1)S(1)}, u32[]{:S(2)}, u32[]{:S(2)}) collective-permute-start(bf16[2,32,1024]{2,1,0:T(8,128)(2,1)S(1)} %get-tuple-element.33), channel_id=1, source_target_pairs={{0,24},{4,28},{8,16},{12,20},{16,8},{20,12},{24,0},{28,4},{1,25},{... | collective-permute-start | bytes 393224 | tf_op jit(solution)/shard_map/ppermute | solution.py:191
  25.6 0.0 collective-permute-start.6
  25.6 0.4 collective-permute-start.9
  26.0 5.0 %product.8 = (bf16[1,64,1024]{2,1,0:T(8,128)(2,1)S(1)}, bf16[1,64,1024]{2,1,0:T(8,128)(2,1)S(1)}, bf16[1,64,1024]{2,1,0:T(8,128)(2,1)S(1)}, bf16[2,64,1024]{2,1,0:T(8,128)(2,1)S(1)}) custom-call(s32[4]{0:T(128)S(1)} %shift-right-arithmetic_xor_fusion.shard, bf16[2,32,1024]{2,1,0:T(8,128)(2,1)S(1)} %copy-done.1, ...), custom_call_target="tpu_custom_call", output_to_operand_aliasing={{3}: (8, {})} | custom-call | flops 1073741824 | bytes 4194304 | tf_op jit(solution)/shard_map/product/pallas_call | solution.py:127
  31.0 1.7 %collective-permute-start.7 = (bf16[2,64,1024]{2,1,0:T(8,128)(2,1)S(1)}, bf16[2,64,1024]{2,1,0:T(8,128)(2,1)S(1)}, u32[]{:S(2)}, u32[]{:S(2)}) collective-permute-start(bf16[2,64,1024]{2,1,0:T(8,128)(2,1)S(1)} %get-tuple-element.37), channel_id=1, source_target_pairs={{0,1},{1,0},{2,3},{3,2},{4,5},{5,4},{6,7},{7,6},{8,9},{9,8},{10,11... | collective-permute-start | bytes 786440 | tf_op jit(solution)/shard_map/ppermute | solution.py:194
  32.6 0.0 collective-permute-done.8
  32.7 2.5 %collective-permute-start.10 = (bf16[1,64,1024]{2,1,0:T(8,128)(2,1)S(1)}, bf16[1,64,1024]{2,1,0:T(8,128)(2,1)S(1)}, u32[]{:S(2)}, u32[]{:S(2)}) collective-permute-start(bf16[1,64,1024]{2,1,0:T(8,128)(2,1)S(1)} %add_convert_fusion.6.refs_3_), channel_id=1, source_target_pairs={{0,3},{1,2},{2,1},{3,0},{4,7},{5,6},{6,5},{7,4},{8,11},{9,10},{10,... | collective-permute-start | bytes 393224 | tf_op jit(solution)/shard_map/ppermute | solution.py:194
  35.2 0.0 collective-permute-done.9
  35.3 1.7 %collective-permute-start.12 = (bf16[1,64,1024]{2,1,0:T(8,128)(2,1)S(1)}, bf16[1,64,1024]{2,1,0:T(8,128)(2,1)S(1)}, u32[]{:S(2)}, u32[]{:S(2)}) collective-permute-start(bf16[1,64,1024]{2,1,0:T(8,128)(2,1)S(1)} %add_convert_fusion.5.refs_4_), channel_id=1, source_target_pairs={{0,3},{1,2},{2,1},{3,0},{4,7},{5,6},{6,5},{7,4},{8,11},{9,10},{10,... | collective-permute-start | bytes 393224 | tf_op jit(solution)/shard_map/ppermute | solution.py:194
  36.9 0.0 collective-permute-done.5.refs_0_.refs_6_
  36.9 0.0 collective-permute-done.6.refs_1_.refs_7_
  36.9 5.6 %product.9.refs_3_ = bf16[2,64,1024]{2,1,0:T(8,128)(2,1)S(1)} custom-call(s32[4]{0:T(128)S(1)} %shift-right-arithmetic_xor_fusion.shard, bf16[2,32,1024]{2,1,0:T(8,128)(2,1)S(1)} %collective-permute-done.5.refs_0_.refs_6_, bf16[2,32,1024]{2,1,0:T(8,128)(2,1)S(1)} %collective-permute-done.6.refs_1_.refs_7_, bf16[1,2,4096,1024]{3,2,1,0:T(8,128)(2,1)} %refs_8_.1, ...), custom_call_target="tpu_custom_call" | custom-call | flops 2147483648 | bytes 8388608 | tf_op jit(solution)/shard_map/product/pallas_call | solution.py:127
  42.6 1.1 %collective-permute-start.18 = (bf16[2,64,1024]{2,1,0:T(8,128)(2,1)S(1)}, bf16[2,64,1024]{2,1,0:T(8,128)(2,1)S(1)}, u32[]{:S(2)}, u32[]{:S(2)}) collective-permute-start(bf16[2,64,1024]{2,1,0:T(8,128)(2,1)S(1)} %product.9.refs_3_), channel_id=1, source_target_pairs={{0,1},{1,0},{2,3},{3,2},{4,5},{5,4},{6,7},{7,6},{8,9},{9,8},{10,11... | collective-permute-start | bytes 786440 | tf_op jit(solution)/shard_map/ppermute | solution.py:194
  43.6 0.0 collective-permute-done.7
  43.7 4.8 %collective-permute-start.15 = (bf16[1,64,1024]{2,1,0:T(8,128)(2,1)S(1)}, bf16[1,64,1024]{2,1,0:T(8,128)(2,1)S(1)}, u32[]{:S(2)}, u32[]{:S(2)}) collective-permute-start(bf16[1,64,1024]{2,1,0:T(8,128)(2,1)S(1)} %add_convert_fusion.7.refs_9_), channel_id=1, source_target_pairs={{0,3},{1,2},{2,1},{3,0},{4,7},{5,6},{6,5},{7,4},{8,11},{9,10},{10,... | collective-permute-start | bytes 393224 | tf_op jit(solution)/shard_map/ppermute | solution.py:194
  48.4 4.0 %product.10.refs_10_ = bf16[1,64,1024]{2,1,0:T(8,128)(2,1)S(1)} custom-call(s32[4]{0:T(128)S(1)} %shift-right-arithmetic_xor_fusion.shard, bf16[2,32,1024]{2,1,0:T(8,128)(2,1)S(1)} %collective-permute-done.5.refs_0_.refs_6_, bf16[2,32,1024]{2,1,0:T(8,128)(2,1)S(1)} %collective-permute-done.6.refs_1_.refs_7_, bf16[1,2,4096,1024]{3,2,1,0:T(8,128)(2,1)} %refs_8_.1, ...), custom_call_target="tpu_custom_call" | custom-call | flops 1073741824 | bytes 4194304 | tf_op jit(solution)/shard_map/product/pallas_call | solution.py:127
  52.5 5.3 %product.11 = (bf16[1,64,1024]{2,1,0:T(8,128)(2,1)S(1)}, bf16[1,64,1024]{2,1,0:T(8,128)(2,1)S(1)}, bf16[1,64,1024]{2,1,0:T(8,128)(2,1)S(1)}, bf16[1,64,1024]{2,1,0:T(8,128)(2,1)S(1)}) custom-call(s32[4]{0:T(128)S(1)} %shift-right-arithmetic_xor_fusion.shard, bf16[2,32,1024]{2,1,0:T(8,128)(2,1)S(1)} %copy-done.1, ...), custom_call_target="tpu_custom_call" | custom-call | flops 1073741824 | bytes 4194304 | tf_op jit(solution)/shard_map/product/pallas_call | solution.py:127
  57.8 0.0 collective-permute-done.10
  57.8 0.1 add_convert_fusion.4
  57.9 0.1 collective-permute-start.11
  58.0 0.1 add_convert_fusion.3
  58.1 0.1 collective-permute-start.19
  58.2 1.6 %collective-permute-start.13 = (bf16[32,1024]{1,0:T(8,128)(2,1)S(1)}, bf16[32,1024]{1,0:T(8,128)(2,1)S(1)}, u32[]{:S(2)}, u32[]{:S(2)}) collective-permute-start(bf16[32,1024]{1,0:T(8,128)(2,1)S(1)} %get-tuple-element.50), channel_id=1, source_target_pairs={{0,8},{4,12},{8,0},{12,4},{16,24},{20,28},{24,16},{28,20},{1,9},{5... | collective-permute-start | bytes 196616 | tf_op jit(solution)/shard_map/ppermute | solution.py:191
  59.8 0.3 collective-permute-start.14
  60.1 5.7 %collective-permute-done.19 = bf16[1,64,1024]{2,1,0:T(8,128)(2,1)S(1)} collective-permute-done((bf16[1,64,1024]{2,1,0:T(8,128)(2,1)S(1)}, bf16[1,64,1024]{2,1,0:T(8,128)(2,1)S(1)}, u32[]{:S(2)}, u32[]{:S(2)}) %collective-permute-start.19) | collective-permute-done | bytes 131104 | tf_op jit(solution)/shard_map/ppermute | solution.py:194
  65.8 0.1 add_convert_fusion
  66.0 1.6 %collective-permute-start.16 = (bf16[32,1024]{1,0:T(8,128)(2,1)S(1)}, bf16[32,1024]{1,0:T(8,128)(2,1)S(1)}, u32[]{:S(2)}, u32[]{:S(2)}) collective-permute-start(bf16[32,1024]{1,0:T(8,128)(2,1)S(1)} %get-tuple-element.48), channel_id=1, source_target_pairs={{0,16},{4,20},{8,24},{12,28},{16,0},{20,4},{24,8},{28,12},{1,17},{... | collective-permute-start | bytes 196616 | tf_op jit(solution)/shard_map/ppermute | solution.py:191
  67.6 2.1 %collective-permute-start.20 = (bf16[32,1024]{1,0:T(8,128)(2,1)S(1)}, bf16[32,1024]{1,0:T(8,128)(2,1)S(1)}, u32[]{:S(2)}, u32[]{:S(2)}) collective-permute-start(bf16[32,1024]{1,0:T(8,128)(2,1)S(1)} %get-tuple-element.46), channel_id=1, source_target_pairs={{0,24},{4,28},{8,16},{12,20},{16,8},{20,12},{24,0},{28,4},{1,25},{... | collective-permute-start | bytes 196616 | tf_op jit(solution)/shard_map/ppermute | solution.py:191
  69.7 0.8 %collective-permute-start.21 = (bf16[32,1024]{1,0:T(8,128)(2,1)S(1)}, bf16[32,1024]{1,0:T(8,128)(2,1)S(1)}, u32[]{:S(2)}, u32[]{:S(2)}) collective-permute-start(bf16[32,1024]{1,0:T(8,128)(2,1)S(1)} %get-tuple-element.45), channel_id=1, source_target_pairs={{0,28},{4,24},{8,20},{12,16},{16,12},{20,8},{24,4},{28,0},{1,29},{... | collective-permute-start | bytes 196616 | tf_op jit(solution)/shard_map/ppermute | solution.py:191
  70.5 1.2 %collective-permute-done.17.refs_5_ = bf16[32,1024]{1,0:T(8,128)(2,1)S(1)} collective-permute-done((bf16[32,1024]{1,0:T(8,128)(2,1)S(1)}, bf16[32,1024]{1,0:T(8,128)(2,1)S(1)}, u32[]{:S(2)}, u32[]{:S(2)}) %collective-permute-start.17) | collective-permute-done | bytes 65568 | tf_op jit(solution)/shard_map/ppermute | solution.py:191
  71.7 1.5 %collective-permute-done.20.refs_6_ = bf16[32,1024]{1,0:T(8,128)(2,1)S(1)} collective-permute-done((bf16[32,1024]{1,0:T(8,128)(2,1)S(1)}, bf16[32,1024]{1,0:T(8,128)(2,1)S(1)}, u32[]{:S(2)}, u32[]{:S(2)}) %collective-permute-start.20) | collective-permute-done | bytes 65568 | tf_op jit(solution)/shard_map/ppermute | solution.py:191
  73.2 1.1 %collective-permute-done.21.refs_7_ = bf16[32,1024]{1,0:T(8,128)(2,1)S(1)} collective-permute-done((bf16[32,1024]{1,0:T(8,128)(2,1)S(1)}, bf16[32,1024]{1,0:T(8,128)(2,1)S(1)}, u32[]{:S(2)}, u32[]{:S(2)}) %collective-permute-start.21) | collective-permute-done | bytes 65568 | tf_op jit(solution)/shard_map/ppermute | solution.py:191
  74.3 1.1 %order.1 = bf16[256,1024]{1,0:T(8,128)(2,1)} custom-call(bf16[256,256]{1,0:T(8,128)(2,1)S(1)} %fusion.refs_11_.place, bf16[32,1024]{1,0:T(8,128)(2,1)S(1)} %get-tuple-element.52.refs_0_, bf16[32,1024]{1,0:T(8,128)(2,1)S(1)} %collective-permute-done.11.refs_1_, bf16[32,1024]{1,0:T(8,128)(2,1)S(1)} %collective-permute-done.13.refs_2_, ...), custom_call_target="tpu_custom_call" | custom-call | tf_op jit(solution)/shard_map/order/pallas_call | solution.py:166
  (28 shorter events, 0.2 us)
Async XLA Ops:
  2.5 14.2 %copy-start.2 = (bf16[2,32,1024]{2,1,0:T(8,128)(2,1)S(1)}, bf16[2,32,1024]{2,1,0:T(8,128)(2,1)}, u32[]{:S(2)}) copy-start(bf16[2,32,1024]{2,1,0:T(8,128)(2,1)} %get-tuple-element.31.refs_5_) | copy-start | bytes 393220
  2.5 5.8 %collective-permute-start = (bf16[2,32,1024]{2,1,0:T(8,128)(2,1)}, bf16[2,32,1024]{2,1,0:T(8,128)(2,1)S(1)}, u32[]{:S(2)}, u32[]{:S(2)}) collective-permute-start(bf16[2,32,1024]{2,1,0:T(8,128)(2,1)} %get-tuple-element.26), channel_id=1, source_target_pairs={{0,4},{4,0},{8,12},{12,8},{16,20},{20,16},{24,28},{28,24},{1,5},{5... | collective-permute-start | bytes 393224 | tf_op jit(solution)/shard_map/ppermute | solution.py:191
  3.0 13.7 %collective-permute-start.1 = (bf16[2,32,1024]{2,1,0:T(8,128)(2,1)}, bf16[2,32,1024]{2,1,0:T(8,128)(2,1)S(1)}, u32[]{:S(2)}, u32[]{:S(2)}) collective-permute-start(bf16[2,32,1024]{2,1,0:T(8,128)(2,1)} %get-tuple-element.27), channel_id=1, source_target_pairs={{0,8},{4,12},{8,0},{12,4},{16,24},{20,28},{24,16},{28,20},{1,9},{5... | collective-permute-start | bytes 393224 | tf_op jit(solution)/shard_map/ppermute | solution.py:191
  5.6 11.1 %collective-permute-start.2 = (bf16[2,32,1024]{2,1,0:T(8,128)(2,1)}, bf16[2,32,1024]{2,1,0:T(8,128)(2,1)S(1)}, u32[]{:S(2)}, u32[]{:S(2)}) collective-permute-start(bf16[2,32,1024]{2,1,0:T(8,128)(2,1)} %get-tuple-element.28), channel_id=1, source_target_pairs={{0,12},{4,8},{8,4},{12,0},{16,28},{20,24},{24,20},{28,16},{1,13},{... | collective-permute-start | bytes 393224 | tf_op jit(solution)/shard_map/ppermute | solution.py:191
  5.7 11.0 %collective-permute-start.3 = (bf16[2,32,1024]{2,1,0:T(8,128)(2,1)}, bf16[2,32,1024]{2,1,0:T(8,128)(2,1)S(1)}, u32[]{:S(2)}, u32[]{:S(2)}) collective-permute-start(bf16[2,32,1024]{2,1,0:T(8,128)(2,1)} %get-tuple-element.29), channel_id=1, source_target_pairs={{0,16},{4,20},{8,24},{12,28},{16,0},{20,4},{24,8},{28,12},{1,17},{... | collective-permute-start | bytes 393224 | tf_op jit(solution)/shard_map/ppermute | solution.py:191
  7.4 9.3 %collective-permute-start.4 = (bf16[2,32,1024]{2,1,0:T(8,128)(2,1)}, bf16[2,32,1024]{2,1,0:T(8,128)(2,1)S(1)}, u32[]{:S(2)}, u32[]{:S(2)}) collective-permute-start(bf16[2,32,1024]{2,1,0:T(8,128)(2,1)} %get-tuple-element.30), channel_id=1, source_target_pairs={{0,20},{4,16},{8,28},{12,24},{16,4},{20,0},{24,12},{28,8},{1,21},{... | collective-permute-start | bytes 393224 | tf_op jit(solution)/shard_map/ppermute | solution.py:191
  8.4 0.9 %copy-start = (bf16[2,32,1024]{2,1,0:T(8,128)(2,1)S(1)}, bf16[2,32,1024]{2,1,0:T(8,128)(2,1)}, u32[]{:S(2)}) copy-start(bf16[2,32,1024]{2,1,0:T(8,128)(2,1)} %get-tuple-element.25.refs_0_) | copy-start | bytes 393220
  9.3 7.5 %copy-start.3 = (bf16[2,32,1024]{2,1,0:T(8,128)(2,1)S(1)}, bf16[2,32,1024]{2,1,0:T(8,128)(2,1)}, u32[]{:S(2)}) copy-start(bf16[2,32,1024]{2,1,0:T(8,128)(2,1)} %get-tuple-element.32.refs_6_) | copy-start | bytes 393220
  9.3 16.7 %copy-start.1 = (bf16[2,32,1024]{2,1,0:T(8,128)(2,1)S(1)}, bf16[2,32,1024]{2,1,0:T(8,128)(2,1)}, u32[]{:S(2)}) copy-start(bf16[2,32,1024]{2,1,0:T(8,128)(2,1)} %get-tuple-element.25.refs_0_) | copy-start | bytes 393220
  14.9 17.7 %collective-permute-start.8 = (bf16[2,64,1024]{2,1,0:T(8,128)(2,1)S(1)}, bf16[2,64,1024]{2,1,0:T(8,128)(2,1)S(1)}, u32[]{:S(2)}, u32[]{:S(2)}) collective-permute-start(bf16[2,64,1024]{2,1,0:T(8,128)(2,1)S(1)} %product.6.refs_7_), channel_id=1, source_target_pairs={{0,1},{1,0},{2,3},{3,2},{4,5},{5,4},{6,7},{7,6},{8,9},{9,8},{10,11... | collective-permute-start | bytes 786440 | tf_op jit(solution)/shard_map/ppermute | solution.py:194
  23.0 13.9 %collective-permute-start.5 = (bf16[2,32,1024]{2,1,0:T(8,128)(2,1)S(1)}, bf16[2,32,1024]{2,1,0:T(8,128)(2,1)S(1)}, u32[]{:S(2)}, u32[]{:S(2)}) collective-permute-start(bf16[2,32,1024]{2,1,0:T(8,128)(2,1)S(1)} %get-tuple-element.33), channel_id=1, source_target_pairs={{0,24},{4,28},{8,16},{12,20},{16,8},{20,12},{24,0},{28,4},{1,25},{... | collective-permute-start | bytes 393224 | tf_op jit(solution)/shard_map/ppermute | solution.py:191
  25.6 11.4 %collective-permute-start.6 = (bf16[2,32,1024]{2,1,0:T(8,128)(2,1)S(1)}, bf16[2,32,1024]{2,1,0:T(8,128)(2,1)S(1)}, u32[]{:S(2)}, u32[]{:S(2)}) collective-permute-start(bf16[2,32,1024]{2,1,0:T(8,128)(2,1)S(1)} %get-tuple-element.34), channel_id=1, source_target_pairs={{0,28},{4,24},{8,20},{12,16},{16,12},{20,8},{24,4},{28,0},{1,29},{... | collective-permute-start | bytes 393224 | tf_op jit(solution)/shard_map/ppermute | solution.py:191
  25.6 9.6 %collective-permute-start.9 = (bf16[2,64,1024]{2,1,0:T(8,128)(2,1)S(1)}, bf16[2,64,1024]{2,1,0:T(8,128)(2,1)S(1)}, u32[]{:S(2)}, u32[]{:S(2)}) collective-permute-start(bf16[2,64,1024]{2,1,0:T(8,128)(2,1)S(1)} %get-tuple-element.40), channel_id=1, source_target_pairs={{0,1},{1,0},{2,3},{3,2},{4,5},{5,4},{6,7},{7,6},{8,9},{9,8},{10,11... | collective-permute-start | bytes 786440 | tf_op jit(solution)/shard_map/ppermute | solution.py:194
  31.0 12.7 %collective-permute-start.7 = (bf16[2,64,1024]{2,1,0:T(8,128)(2,1)S(1)}, bf16[2,64,1024]{2,1,0:T(8,128)(2,1)S(1)}, u32[]{:S(2)}, u32[]{:S(2)}) collective-permute-start(bf16[2,64,1024]{2,1,0:T(8,128)(2,1)S(1)} %get-tuple-element.37), channel_id=1, source_target_pairs={{0,1},{1,0},{2,3},{3,2},{4,5},{5,4},{6,7},{7,6},{8,9},{9,8},{10,11... | collective-permute-start | bytes 786440 | tf_op jit(solution)/shard_map/ppermute | solution.py:194
  32.7 25.1 %collective-permute-start.10 = (bf16[1,64,1024]{2,1,0:T(8,128)(2,1)S(1)}, bf16[1,64,1024]{2,1,0:T(8,128)(2,1)S(1)}, u32[]{:S(2)}, u32[]{:S(2)}) collective-permute-start(bf16[1,64,1024]{2,1,0:T(8,128)(2,1)S(1)} %add_convert_fusion.6.refs_3_), channel_id=1, source_target_pairs={{0,3},{1,2},{2,1},{3,0},{4,7},{5,6},{6,5},{7,4},{8,11},{9,10},{10,... | collective-permute-start | bytes 393224 | tf_op jit(solution)/shard_map/ppermute | solution.py:194
  35.3 22.7 %collective-permute-start.12 = (bf16[1,64,1024]{2,1,0:T(8,128)(2,1)S(1)}, bf16[1,64,1024]{2,1,0:T(8,128)(2,1)S(1)}, u32[]{:S(2)}, u32[]{:S(2)}) collective-permute-start(bf16[1,64,1024]{2,1,0:T(8,128)(2,1)S(1)} %add_convert_fusion.5.refs_4_), channel_id=1, source_target_pairs={{0,3},{1,2},{2,1},{3,0},{4,7},{5,6},{6,5},{7,4},{8,11},{9,10},{10,... | collective-permute-start | bytes 393224 | tf_op jit(solution)/shard_map/ppermute | solution.py:194
  42.6 15.4 %collective-permute-start.18 = (bf16[2,64,1024]{2,1,0:T(8,128)(2,1)S(1)}, bf16[2,64,1024]{2,1,0:T(8,128)(2,1)S(1)}, u32[]{:S(2)}, u32[]{:S(2)}) collective-permute-start(bf16[2,64,1024]{2,1,0:T(8,128)(2,1)S(1)} %product.9.refs_3_), channel_id=1, source_target_pairs={{0,1},{1,0},{2,3},{3,2},{4,5},{5,4},{6,7},{7,6},{8,9},{9,8},{10,11... | collective-permute-start | bytes 786440 | tf_op jit(solution)/shard_map/ppermute | solution.py:194
  43.7 16.4 %collective-permute-start.15 = (bf16[1,64,1024]{2,1,0:T(8,128)(2,1)S(1)}, bf16[1,64,1024]{2,1,0:T(8,128)(2,1)S(1)}, u32[]{:S(2)}, u32[]{:S(2)}) collective-permute-start(bf16[1,64,1024]{2,1,0:T(8,128)(2,1)S(1)} %add_convert_fusion.7.refs_9_), channel_id=1, source_target_pairs={{0,3},{1,2},{2,1},{3,0},{4,7},{5,6},{6,5},{7,4},{8,11},{9,10},{10,... | collective-permute-start | bytes 393224 | tf_op jit(solution)/shard_map/ppermute | solution.py:194
  57.9 9.8 %collective-permute-start.11 = (bf16[32,1024]{1,0:T(8,128)(2,1)S(1)}, bf16[32,1024]{1,0:T(8,128)(2,1)S(1)}, u32[]{:S(2)}, u32[]{:S(2)}) collective-permute-start(bf16[32,1024]{1,0:T(8,128)(2,1)S(1)} %get-tuple-element.51), channel_id=1, source_target_pairs={{0,4},{4,0},{8,12},{12,8},{16,20},{20,16},{24,28},{28,24},{1,5},{5... | collective-permute-start | bytes 196616 | tf_op jit(solution)/shard_map/ppermute | solution.py:191
  58.1 7.8 %collective-permute-start.19 = (bf16[1,64,1024]{2,1,0:T(8,128)(2,1)S(1)}, bf16[1,64,1024]{2,1,0:T(8,128)(2,1)S(1)}, u32[]{:S(2)}, u32[]{:S(2)}) collective-permute-start(bf16[1,64,1024]{2,1,0:T(8,128)(2,1)S(1)} %add_convert_fusion.1), channel_id=1, source_target_pairs={{0,3},{1,2},{2,1},{3,0},{4,7},{5,6},{6,5},{7,4},{8,11},{9,10},{10,... | collective-permute-start | bytes 393224 | tf_op jit(solution)/shard_map/ppermute | solution.py:194
  58.2 11.5 %collective-permute-start.13 = (bf16[32,1024]{1,0:T(8,128)(2,1)S(1)}, bf16[32,1024]{1,0:T(8,128)(2,1)S(1)}, u32[]{:S(2)}, u32[]{:S(2)}) collective-permute-start(bf16[32,1024]{1,0:T(8,128)(2,1)S(1)} %get-tuple-element.50), channel_id=1, source_target_pairs={{0,8},{4,12},{8,0},{12,4},{16,24},{20,28},{24,16},{28,20},{1,9},{5... | collective-permute-start | bytes 196616 | tf_op jit(solution)/shard_map/ppermute | solution.py:191
  59.8 10.8 %collective-permute-start.14 = (bf16[32,1024]{1,0:T(8,128)(2,1)S(1)}, bf16[32,1024]{1,0:T(8,128)(2,1)S(1)}, u32[]{:S(2)}, u32[]{:S(2)}) collective-permute-start(bf16[32,1024]{1,0:T(8,128)(2,1)S(1)} %get-tuple-element.49), channel_id=1, source_target_pairs={{0,12},{4,8},{8,4},{12,0},{16,28},{20,24},{24,20},{28,16},{1,13},{... | collective-permute-start | bytes 196616 | tf_op jit(solution)/shard_map/ppermute | solution.py:191
  66.0 4.6 %collective-permute-start.16 = (bf16[32,1024]{1,0:T(8,128)(2,1)S(1)}, bf16[32,1024]{1,0:T(8,128)(2,1)S(1)}, u32[]{:S(2)}, u32[]{:S(2)}) collective-permute-start(bf16[32,1024]{1,0:T(8,128)(2,1)S(1)} %get-tuple-element.48), channel_id=1, source_target_pairs={{0,16},{4,20},{8,24},{12,28},{16,0},{20,4},{24,8},{28,12},{1,17},{... | collective-permute-start | bytes 196616 | tf_op jit(solution)/shard_map/ppermute | solution.py:191
  67.6 4.1 %collective-permute-start.17 = (bf16[32,1024]{1,0:T(8,128)(2,1)S(1)}, bf16[32,1024]{1,0:T(8,128)(2,1)S(1)}, u32[]{:S(2)}, u32[]{:S(2)}) collective-permute-start(bf16[32,1024]{1,0:T(8,128)(2,1)S(1)} %get-tuple-element.47), channel_id=1, source_target_pairs={{0,20},{4,16},{8,28},{12,24},{16,4},{20,0},{24,12},{28,8},{1,21},{... | collective-permute-start | bytes 196616 | tf_op jit(solution)/shard_map/ppermute | solution.py:191
  67.6 5.5 %collective-permute-start.20 = (bf16[32,1024]{1,0:T(8,128)(2,1)S(1)}, bf16[32,1024]{1,0:T(8,128)(2,1)S(1)}, u32[]{:S(2)}, u32[]{:S(2)}) collective-permute-start(bf16[32,1024]{1,0:T(8,128)(2,1)S(1)} %get-tuple-element.46), channel_id=1, source_target_pairs={{0,24},{4,28},{8,16},{12,20},{16,8},{20,12},{24,0},{28,4},{1,25},{... | collective-permute-start | bytes 196616 | tf_op jit(solution)/shard_map/ppermute | solution.py:191
  69.7 4.6 %collective-permute-start.21 = (bf16[32,1024]{1,0:T(8,128)(2,1)S(1)}, bf16[32,1024]{1,0:T(8,128)(2,1)S(1)}, u32[]{:S(2)}, u32[]{:S(2)}) collective-permute-start(bf16[32,1024]{1,0:T(8,128)(2,1)S(1)} %get-tuple-element.45), channel_id=1, source_target_pairs={{0,28},{4,24},{8,20},{12,16},{16,12},{20,8},{24,4},{28,0},{1,29},{... | collective-permute-start | bytes 196616 | tf_op jit(solution)/shard_map/ppermute | solution.py:191
